TPU v7x, 256 devices: a whole 4x4x8 slice. The times are simulated.
256 devices in a mesh: dp: 16 (over x_lo, y, core), expert: 16 (over x_hi, z).
Axes of the slice: x: 4 (x_hi: 2, x_lo: 2; x = x_hi * 2 + x_lo), y: 4, z: 8, core: 2. Of those that a mesh axis runs over, the one named last changes fastest.
Arguments:
- out_grad: bfloat16 [32768, 5120], P(('dp', 'expert')), may hold values from -6 to 6
- expert_ids: int32 [32768, 1], P(('dp', 'expert')), may hold values from 0 to 15; in each aligned block of 128 rows (0 to 127, 128 to 255, ...) at most 10 rows name the same one
- router_logit: float32 [32768], P(('dp', 'expert')), may hold values from -8 to 8
- hidden_saved: bfloat16 [16, 2560, 4096], P('expert', None, 'dp'), may hold values from -60 to 60
- down_weight: bfloat16 [16, 4096, 5120], P('expert', 'dp'), may hold values from -0.09375 to 0.09375
Outputs:
- weight_grad: bfloat16 [16, 4096, 5120], P('expert', 'dp')
- logit_grad: float32 [32768], P(('dp', 'expert'))
Inputs may be any that keep to these rules, and one draw needn't show every extreme that they name: `expert_ids`: within the 128 rows of one device no expert is named more than 10 times; some expert is named exactly 10 times there in every draw.
All inputs are finite; a program needn't handle non-finite values.
Results may differ from a plain program's by a relative error of at most 0.0055.
Values may be sent and summed in bfloat16 or wider, within the bound.
No kernel may reach another device: no remote copies, remote signals or barrier semaphores. Data moves between devices by JAX's collectives and lax.ppermute only.
A program may use at most 128 MiB of HBM per device.

v0:
```python
import jax
import jax.numpy as jnp
import numpy as np
from jax import lax
from jax.experimental import pallas as pl
from jax.experimental.pallas import tpu as pltpu
from jax.sharding import Mesh, PartitionSpec as P

BF = jnp.bfloat16
F32 = jnp.float32
CAP = 10
TOK = 128
CHUNKS = (1280, 1280)
HALF = 2560
FD = 256
BLOCK = 320
QUARTER = 1280
TOP = 160
SLOTS = 2560
MIB = 1 << 20
AXES = ("x_lo", "y", "core", "x_hi", "z")
VMEM = pl.BlockSpec(memory_space=pltpu.VMEM)
SMEM = pl.BlockSpec(memory_space=pltpu.SMEM)
ANY = pl.BlockSpec(memory_space=pl.ANY)


def pair_targets():
    i = np.arange(2 * BLOCK)
    y, core, x_hi, z, r = i // 320, i // 160 % 2, i // 80 % 2, i // 10 % 8, i % 10
    return (y * 320 + z * 40 + core * 20 + x_hi * 10 + r).astype(np.int32)


def route_kernel(ids_ref, logit_ref, out_ref):
    ids = ids_ref[...].astype(F32)
    row = lax.broadcasted_iota(jnp.int32, (TOK, TOK), 0)
    col = lax.broadcasted_iota(jnp.int32, (TOK, TOK), 1)
    ids_row = jnp.sum(jnp.where(row == col, ids, 0.0), axis=0, keepdims=True)
    rank = jnp.sum(jnp.where((ids == ids_row) & (row < col), 1.0, 0.0), axis=0, keepdims=True)
    prob = jax.nn.sigmoid(logit_ref[...]).astype(BF).astype(F32)
    out_ref[...] = jnp.concatenate([ids_row, rank, prob, jnp.zeros((5, TOK), F32)], axis=0)


def route(ids, logit):
    return pl.pallas_call(
        route_kernel,
        out_shape=jax.ShapeDtypeStruct((8, TOK), F32),
        in_specs=[VMEM, VMEM],
        out_specs=VMEM,
        name="route",
    )(ids, logit.reshape(1, TOK))


def place_kernel(where_ref, m0, m1, m2, m3, t0, t1, t2, t3, out_ref, toks, sems):
    copies = [pltpu.make_async_copy(t, toks.at[i], sems.at[i]) for i, t in enumerate((t0, t1, t2, t3))]
    for copy in copies:
        copy.start()
    core, x_hi = where_ref[0], where_ref[1]
    slot = lax.broadcasted_iota(jnp.int32, (BLOCK, TOK), 0).astype(F32)
    first = (8 * x_hi).astype(F32)
    hots = []
    for meta, other_core, other_x in ((m0, 0, 0), (m1, 1, 0), (m2, 0, 1), (m3, 1, 1)):
        src_core = core if other_core == 0 else 1 - core
        src_x = x_hi if other_x == 0 else 1 - x_hi
        base = (src_core * 20 + src_x * 10).astype(F32)
        z = meta[0:1, :] - first
        pos = jnp.where((z >= 0.0) & (z < 8.0), z * 40.0 + meta[1:2, :] + base, -1.0)
        hots.append(jnp.where(slot == pos, meta[2:3, :], 0.0).astype(BF))
    for copy in copies:
        copy.wait()
    total = None
    for i in range(2):
        hot = jnp.concatenate(hots[2 * i : 2 * i + 2], axis=1)
        pair = toks[2 * i : 2 * i + 2].reshape(2 * TOK, toks.shape[2])
        part = jnp.dot(hot, pair, preferred_element_type=F32)
        total = part if total is None else total + part
    out_ref[...] = total.astype(BF)


def place(where, metas, toks):
    width = toks[0].shape[1]
    return pl.pallas_call(
        place_kernel,
        out_shape=jax.ShapeDtypeStruct((BLOCK, width), BF),
        in_specs=[SMEM] + [VMEM] * 4 + [ANY] * 4,
        out_specs=VMEM,
        scratch_shapes=[pltpu.VMEM((4, TOK, width), BF), pltpu.SemaphoreType.DMA((4,))],
        compiler_params=pltpu.CompilerParams(vmem_limit_bytes=16 * MIB),
        cost_estimate=pl.CostEstimate(
            flops=2 * 4 * BLOCK * TOK * width, bytes_accessed=2 * width * (4 * TOK + BLOCK), transcendentals=0
        ),
        name="place",
    )(where, *metas, *toks)


def turn_kernel(where_ref, target_ref, own_ref, par_ref, out_ref, hot_ref):
    col = lax.broadcasted_iota(jnp.int32, (2 * BLOCK, 2 * BLOCK), 1)
    hot_ref[...] = jnp.where(col == target_ref[...], 1.0, 0.0).astype(BF)
    for x in range(2):
        for pair in range(2):
            for half, ref in enumerate((own_ref, par_ref)):
                runs = []
                for y in (2 * pair, 2 * pair + 1):
                    for core in range(2):
                        for x_hi in range(2):
                            same = where_ref[1] if x_hi else 1 - where_ref[1]
                            x_lo = x * same + (1 - x) * (1 - same)
                            start = ((x_lo * 4 + y) * 2 + core) * 160 + x_hi * 80
                            runs.append(ref[pl.ds(pl.multiple_of(start, 16), 80), :])
                rows = jnp.concatenate(runs, axis=0)
                turned = lax.dot_general(rows, hot_ref[...], (((0,), (0,)), ((), ())), preferred_element_type=F32)
                at = pl.ds(x * HALF // 2 + pair * 2 * BLOCK, 2 * BLOCK)
                out_ref[pl.ds(half * FD, FD), at] = turned.astype(BF)


def turn(where, target, own, par):
    return pl.pallas_call(
        turn_kernel,
        out_shape=jax.ShapeDtypeStruct((2 * FD, SLOTS), BF),
        in_specs=[SMEM] + [VMEM] * 3,
        out_specs=VMEM,
        scratch_shapes=[pltpu.VMEM((2 * BLOCK, 2 * BLOCK), BF)],
        compiler_params=pltpu.CompilerParams(vmem_limit_bytes=24 * MIB),
        cost_estimate=pl.CostEstimate(flops=2 * 2 * FD * SLOTS * 2 * BLOCK, bytes_accessed=5 * MIB, transcendentals=0),
        name="turn",
    )(where, target, own, par)


def expert_kernel(off, width, places, sides, grad, where_ref, *refs):
    n = len(places)
    pieces, (hid_ref, down_ref, par_ref), refs = refs[:n], refs[n : n + 3], refs[n + 3 :]
    outs, (rows, own_wts, sems) = refs[:-3], refs[-3:]
    core, y, x_lo = where_ref[0], where_ref[2], where_ref[3]

    def place_of(side):
        return x_lo if side == 0 else 1 - x_lo

    copies = []
    start = pl.multiple_of(core * HALF + off, 128)
    copies.append((None, pltpu.make_async_copy(down_ref.at[:, pl.ds(start, width)], own_wts, sems.at[n])))
    for i, (ref, (side, up)) in enumerate(zip(pieces, places)):
        start = pl.multiple_of(place_of(side) * QUARTER + lax.rem(y + up, 4) * BLOCK, BLOCK)
        copies.append((side, pltpu.make_async_copy(ref, rows.at[pl.ds(start, BLOCK), :], sems.at[i])))
    copies.sort(key=lambda c: c[0] in sides or c[0] is None, reverse=True)
    for _, copy in copies:
        copy.start()
    for side, copy in copies:
        if side in sides or side is None:
            copy.wait()

    tile = QUARTER // 2
    for k, side in enumerate(sides):

        @pl.loop(0, 2)
        def _(i):
            at = pl.ds(pl.multiple_of(place_of(side) * QUARTER + i * tile, 128), tile)
            total = None
            for half in range(2):
                wts = own_wts[...] if half == 0 else par_ref[:, pl.ds(off, width)]
                back = lax.dot_general(wts, rows[at, :], (((1,), (1,)), ((), ())), preferred_element_type=F32)
                part = jnp.sum(back * hid_ref[pl.ds(half * FD, FD), at].astype(F32), axis=0, keepdims=True)
                total = part if total is None else total + part
            outs[-1][k : k + 1, pl.ds(pl.multiple_of(i * tile, 128), tile)] = total

    for side, copy in copies:
        if not (side in sides or side is None):
            copy.wait()
    if grad:
        for i in range(2):
            at = pl.ds(i * FD, FD)
            outs[i][...] = jnp.dot(hid_ref[at, :], rows[...], preferred_element_type=F32).astype(BF)


def expert_part(where, pieces, hid, down, par, off, width, places, sides=(0, 1), grad=True):
    grads = (jax.ShapeDtypeStruct((FD, width), BF),) * 2 if grad else ()
    shapes = grads + (jax.ShapeDtypeStruct((len(sides), QUARTER), F32),)
    return pl.pallas_call(
        lambda *refs: expert_kernel(off, width, places, sides, grad, *refs),
        out_shape=shapes,
        in_specs=[SMEM] + [ANY] * len(pieces) + [VMEM, ANY, VMEM],
        out_specs=(VMEM,) * len(shapes),
        scratch_shapes=[
            pltpu.VMEM((SLOTS, width), BF),
            pltpu.VMEM((FD, width), BF),
            pltpu.SemaphoreType.DMA((len(pieces) + 1,)),
        ],
        compiler_params=pltpu.CompilerParams(vmem_limit_bytes=28 * MIB),
        cost_estimate=pl.CostEstimate(
            flops=2 * (len(sides) + 2 * grad) * FD * SLOTS * width,
            bytes_accessed=2 * SLOTS * (width + 2 * FD),
            transcendentals=0,
        ),
        name="expert_part",
    )(where, *pieces, hid, down, par)


def join_kernel(n, where_ref, *refs):
    own, got, out_ref, sems = refs[:n], refs[n : 2 * n], refs[2 * n], refs[2 * n + 1]
    core = where_ref[0]
    copies = []
    for refs_of, side in ((own, core), (got, 1 - core)):
        off = 0
        for ref in refs_of:
            width = ref.shape[1]
            start = pl.multiple_of(side * HALF + off, 128)
            copy = pltpu.make_async_copy(ref, out_ref.at[:, pl.ds(start, width)], sems.at[len(copies)])
            copy.start()
            copies.append(copy)
            off += width
    for copy in copies:
        copy.wait()


def join(where, own, got):
    n = len(own)
    return pl.pallas_call(
        lambda *refs: join_kernel(n, *refs),
        out_shape=jax.ShapeDtypeStruct((FD, 2 * HALF), BF),
        in_specs=[SMEM] + [ANY] * (2 * n),
        out_specs=VMEM,
        scratch_shapes=[pltpu.SemaphoreType.DMA((2 * n,))],
        compiler_params=pltpu.CompilerParams(vmem_limit_bytes=16 * MIB),
        name="join",
    )(where, *own, *got)


def tie(array, other):
    return lax.optimization_barrier((array, other))


def ring(axis, shift):
    def send(array):
        size = lax.axis_size(axis)
        return lax.ppermute(array, axis, [(i, (i + shift) % size) for i in range(size)])

    return send


def swap_x(core_too):
    axes = ("x_lo", "core", "x_hi")
    flip = 7 if core_too else 5

    def send(array):
        return lax.ppermute(array, axes, [(i, i ^ flip) for i in range(8)])

    return send


def body(out_grad, expert_ids, router_logit, hidden_saved, down_weight):
    core, x_hi = lax.axis_index("core"), lax.axis_index("x_hi")
    y, x_lo = lax.axis_index("y"), lax.axis_index("x_lo")
    where = jnp.stack([core, x_hi, y, x_lo]).astype(jnp.int32)
    swap_core, swap_xx, swap_xc = ring("core", 1), swap_x(False), swap_x(True)
    up, down, cross = ring("y", 1), ring("y", 3), ring("x_lo", 1)
    first = core == 0
    hidden = hidden_saved[0]
    down_own = down_weight[0]

    offs = [sum(CHUNKS[:k]) for k in range(len(CHUNKS))]
    n = len(CHUNKS)
    meta = route(expert_ids, router_logit)
    metas = (meta, swap_core(meta), swap_xx(meta), swap_xc(meta))
    own_tok, oth_tok = [], []
    for off, width in zip(offs, CHUNKS):
        low, high = out_grad[:, off : off + width], out_grad[:, HALF + off : HALF + off + width]
        own_tok.append(jnp.where(first, low, high))
        oth_tok.append(jnp.where(first, high, low))

    hidden_par = swap_core(hidden)
    down_par = swap_core(jnp.where(first, down_own[:, HALF:], down_own[:, :HALF]))
    target = jnp.asarray(pair_targets())
    hid = turn(where, target.reshape(2 * BLOCK, 1), hidden, hidden_par)

    def fetch(own, oth):
        return own, swap_core(oth), swap_xx(own), swap_xc(oth)

    def spread(sent):
        width = sent.shape[1]
        got = lax.all_to_all(sent.reshape(8, 40, width), "z", split_axis=0, concat_axis=0, tiled=True)
        return got.reshape(BLOCK, width)

    own, oth = own_tok[0], oth_tok[0]
    tok_0 = fetch(own, oth)
    (own, oth), tok_0 = tie((own_tok[1], oth_tok[1]), tok_0)
    tok_1 = fetch(own, oth)
    rows_0 = spread(place(where, metas, tok_0))
    sent_1, rows_0 = tie(place(where, metas, tok_1), rows_0)
    rows_1 = spread(sent_1)

    below_0, above_0, over_0 = up(rows_0), down(rows_0), cross(rows_0)
    far_0 = up(below_0)
    over_below_0, over_above_0 = up(over_0), down(over_0)
    over_far_0 = cross(far_0)
    rows, (below_0, above_0, hid) = tie(rows_1, (below_0, above_0, hid))
    over_1, above_1 = cross(rows), down(rows)
    rows, far_0 = tie(rows, far_0)
    below_1 = up(rows)
    far_1 = down(above_1)
    over_below_1, over_above_1 = up(over_1), down(over_1)
    whole = tuple((side, up_by) for side in range(2) for up_by in (0, 3, 1, 2))
    pieces = (rows_0, below_0, above_0, far_0, over_0, over_below_0, over_above_0, over_far_0)
    common = (hid, down_own, down_par)
    own_0, oth_0, score_0 = expert_part(where, pieces, *common, 0, CHUNKS[0], whole)
    far_1, score_0 = tie(far_1, score_0)
    over_far_1 = cross(far_1)
    pieces = (rows_1, below_1, above_1, far_1, over_1, over_below_1, over_above_1, over_far_1)
    (score_1,) = expert_part(where, pieces[:4], *common, CHUNKS[0], CHUNKS[1], whole[:4], sides=(0,), grad=False)
    own_1, oth_1, score_2 = expert_part(where, pieces, *common, CHUNKS[0], CHUNKS[1], whole, sides=(1,))
    weight_grad = join(where, (own_0, own_1), (swap_core(oth_0), swap_core(oth_1)))[None]

    score = (score_0 + jnp.concatenate([score_1, score_2], axis=0)).reshape(2, 4, BLOCK)
    score = jnp.where(x_lo == 0, score, score[::-1])
    spot = (target[:BLOCK, None] == jnp.arange(BLOCK, dtype=jnp.int32)[None, :]).astype(F32)
    turned = lax.dot_general(
        score.reshape(8, BLOCK), spot, (((1,), (1,)), ((), ())), precision=lax.Precision.HIGHEST,
        preferred_element_type=F32,
    ).reshape(2, 4, 2, 2, 80)
    same = (jnp.arange(2) == x_hi).reshape(1, 1, 1, 2, 1)
    parts = jnp.where(same, turned, turned[::-1]).reshape(16, 160)
    mine = lax.all_to_all(parts, ("x_lo", "y", "core"), split_axis=0, concat_axis=0, tiled=True)
    own_scores = jnp.sum(mine, axis=0).reshape(16, CAP)
    back = lax.all_to_all(own_scores, ("x_hi", "z"), split_axis=0, concat_axis=0, tiled=True)
    back, weight_grad = tie(back, weight_grad)
    slot = (meta[0] * CAP + meta[1]).astype(jnp.int32)
    hit = slot[:, None] == jnp.arange(16 * CAP, dtype=jnp.int32)[None, :]
    token_scores = jnp.sum(jnp.where(hit, back.reshape(1, 16 * CAP), 0.0), axis=1)
    prob = jax.nn.sigmoid(router_logit)
    logit_grad = prob * (1.0 - prob) / meta[2] * token_scores
    return weight_grad, logit_grad


def solution(mesh):
    fine = Mesh(mesh.devices.reshape(2, 4, 2, 2, 8), AXES)
    dp, expert = ("x_lo", "y", "core"), ("x_hi", "z")
    placed = (
        P(AXES, None),
        P(AXES, None),
        P(AXES),
        P(expert, None, dp),
        P(expert, dp, None),
    )
    return jax.shard_map(
        body,
        mesh=fine,
        in_specs=placed,
        out_specs=(P(expert, dp, None), P(AXES)),
        check_vma=False,
    )
```

profile of v0, /device:TPU:1, one launch (start us, length us, event | category | flops | bytes accessed | tf_op | source)
XLA Modules:
  0.0 203.9 jit_solution(3565782648314698229)
XLA Ops:
  0.6 1.4 broadcast_select_fusion
  2.0 3.3 %collective-permute-start.3 = (bf16[128,1280]{1,0:T(8,128)(2,1)S(1)}, bf16[128,1280]{1,0:T(8,128)(2,1)S(1)}, u32[]{:S(2)}, u32[]{:S(2)}) collective-permute-start(bf16[128,1280]{1,0:T(8,128)(2,1)S(1)} %get-tuple-element.50), channel_id=1, source_target_pairs={{0,16},{16,0},{1,17},{17,1},{2,18},{18,2},{3,19},{19,3},{4,20},{20... | collective-permute-start | bytes 983048 | tf_op jit(solution)/shard_map/ppermute | solution.py:233
  5.3 0.8 collective-permute-start.4
  6.1 2.2 %collective-permute-start.5 = (bf16[128,1280]{1,0:T(8,128)(2,1)S(1)}, bf16[128,1280]{1,0:T(8,128)(2,1)S(1)}, u32[]{:S(2)}, u32[]{:S(2)}) collective-permute-start(bf16[128,1280]{1,0:T(8,128)(2,1)S(1)} %get-tuple-element.50), channel_id=1, source_target_pairs={{0,152},{8,144},{16,136},{24,128},{128,24},{136,16},{144,8},{152,0... | collective-permute-start | bytes 983048 | tf_op jit(solution)/shard_map/ppermute | solution.py:243
  8.3 0.7 copy.15.ids_ref
  9.0 1.5 route.1.m0
  10.6 0.1 collective-permute-start
  10.7 0.7 collective-permute-start.1
  11.5 2.5 %collective-permute-start.2 = (f32[8,128]{1,0:T(8,128)}, f32[8,128]{1,0:T(8,128)S(1)}, u32[]{:S(2)}, u32[]{:S(2)}) collective-permute-start(f32[8,128]{1,0:T(8,128)} %route.1.m0), channel_id=1, source_target_pairs={{0,152},{8,144},{16,136},{24,128},{128,24},{136,16},{144,8},{152,0... | collective-permute-start | bytes 12296 | tf_op jit(solution)/shard_map/ppermute | solution.py:243
  14.0 1.8 collective-permute-done.4.t2
  15.8 7.3 %collective-permute-done.5.t3 = bf16[128,1280]{1,0:T(8,128)(2,1)S(1)} collective-permute-done((bf16[128,1280]{1,0:T(8,128)(2,1)S(1)}, bf16[128,1280]{1,0:T(8,128)(2,1)S(1)}, u32[]{:S(2)}, u32[]{:S(2)}) %collective-permute-start.5) | collective-permute-done | bytes 327712 | tf_op jit(solution)/shard_map/ppermute | solution.py:243
  23.1 0.3 collective-permute-done.2.m3
  23.5 0.7 copy-done.11
  24.1 2.5 %place.3 = bf16[320,1280]{1,0:T(8,128)(2,1)} custom-call(s32[4]{0:T(128)S(1)} %pad_add_fusion.where_ref.refs_0_, f32[8,128]{1,0:T(8,128)S(1)} %copy-done.11, f32[8,128]{1,0:T(8,128)S(1)} %collective-permute-done.m1, f32[8,128]{1,0:T(8,128)S(1)} %collective-permute-done.1.m2, f32[8,128]{1,0:T(8,128)S(1)} %collective-permute-done.2.m3, ...), custom_call_target="tpu_custom_call" | custom-call | flops 419430400 | bytes 2129920 | tf_op jit(solution)/shard_map/place/pallas_call | solution.py:81
  26.7 6.5 %all-to-all-start = ((bf16[8,40,1280]{2,1,0:T(8,128)(2,1)}), bf16[8,40,1280]{2,1,0:T(8,128)(2,1)}, u32[]{:S(2)}, u32[]{:S(2)}) async-start(bf16[8,40,1280]{2,1,0:T(8,128)(2,1)} %bitcast.5), calls=%async_computation | async-start | bytes 1638400 | tf_op jit(solution)/shard_map/all_to_all | solution.py:278
  33.1 0.7 collective-permute-start.6
  33.8 2.5 %collective-permute-start.7 = (bf16[128,1280]{1,0:T(8,128)(2,1)S(1)}, bf16[128,1280]{1,0:T(8,128)(2,1)S(1)}, u32[]{:S(2)}, u32[]{:S(2)}) collective-permute-start(bf16[128,1280]{1,0:T(8,128)(2,1)S(1)} %get-tuple-element.26.t0), channel_id=1, source_target_pairs={{0,136},{8,128},{16,152},{24,144},{128,8},{136,0},{144,24},{152,16... | collective-permute-start | bytes 983048 | tf_op jit(solution)/shard_map/ppermute | solution.py:243
  36.3 0.4 collective-permute-start.8
  36.7 0.1 collective-permute-start.11
  36.9 7.5 %collective-permute-done.7.t2 = bf16[128,1280]{1,0:T(8,128)(2,1)S(1)} collective-permute-done((bf16[128,1280]{1,0:T(8,128)(2,1)S(1)}, bf16[128,1280]{1,0:T(8,128)(2,1)S(1)}, u32[]{:S(2)}, u32[]{:S(2)}) %collective-permute-start.7) | collective-permute-done | bytes 327712 | tf_op jit(solution)/shard_map/ppermute | solution.py:243
  44.4 7.1 %collective-permute-done.8.t3 = bf16[128,1280]{1,0:T(8,128)(2,1)S(1)} collective-permute-done((bf16[128,1280]{1,0:T(8,128)(2,1)S(1)}, bf16[128,1280]{1,0:T(8,128)(2,1)S(1)}, u32[]{:S(2)}, u32[]{:S(2)}) %collective-permute-start.8) | collective-permute-done | bytes 327712 | tf_op jit(solution)/shard_map/ppermute | solution.py:243
  51.5 1.6 place.2
  53.1 0.9 copy-done.1
  54.0 3.5 %all-to-all-done = bf16[8,40,1280]{2,1,0:T(8,128)(2,1)} async-done(((bf16[8,40,1280]{2,1,0:T(8,128)(2,1)}), bf16[8,40,1280]{2,1,0:T(8,128)(2,1)}, u32[]{:S(2)}, u32[]{:S(2)}) %all-to-all-start) | async-done | bytes 819232 | tf_op jit(solution)/shard_map/all_to_all | solution.py:278
  57.5 1.3 collective-permute-start.9
  58.8 3.8 %all-to-all-start.1 = ((bf16[8,40,1280]{2,1,0:T(8,128)(2,1)}), bf16[8,40,1280]{2,1,0:T(8,128)(2,1)S(1)}, u32[]{:S(2)}, u32[]{:S(2)}) async-start(bf16[8,40,1280]{2,1,0:T(8,128)(2,1)} %bitcast.35), calls=%async_computation.1 | async-start | bytes 1638400 | tf_op jit(solution)/shard_map/all_to_all | solution.py:278
  62.6 1.2 slice_select_fusion
  63.8 0.5 collective-permute-start.19
  64.4 1.4 collective-permute-start.10
  65.7 12.7 %collective-permute-done.9.refs_2_ = bf16[320,1280]{1,0:T(8,128)(2,1)} collective-permute-done((bf16[320,1280]{1,0:T(8,128)(2,1)}, bf16[320,1280]{1,0:T(8,128)(2,1)}, u32[]{:S(2)}, u32[]{:S(2)}) %collective-permute-start.9) | collective-permute-done | bytes 819232 | tf_op jit(solution)/shard_map/ppermute | solution.py:233
  78.5 4.4 %turn.1.refs_9_.refs_5_ = bf16[512,2560]{1,0:T(8,128)(2,1)S(1)} custom-call(s32[4]{0:T(128)S(1)} %pad_add_fusion.where_ref.refs_0_, s32[640,1]{1,0:T(8,128)S(1)} %copy-done.16, bf16[2560,256]{1,0:T(8,128)(2,1)} %bitcast.9.own_ref, bf16[2560,256]{1,0:T(8,128)(2,1)} %collective-permute-done.11.par_ref), custom_call_target="tpu_custom_call" | custom-call | flops 1677721600 | bytes 5242880 | tf_op jit(solution)/shard_map/turn/pallas_call | solution.py:116
  82.9 1.5 copy-done.2
  84.6 0.9 copy-done.13
  85.5 1.5 all-to-all-done.1
  86.9 1.4 collective-permute-start.12
  88.4 2.7 %collective-permute-start.17 = (bf16[320,1280]{1,0:T(8,128)(2,1)}, bf16[320,1280]{1,0:T(8,128)(2,1)S(1)}, u32[]{:S(2)}, u32[]{:S(2)}) collective-permute-start(bf16[320,1280]{1,0:T(8,128)(2,1)} %collective-permute-done.15.refs_5_), channel_id=1, source_target_pairs={{0,96},{32,0},{64,32},{96,64},{1,97},{33,1},{65,33},{97,65},{2,98}... | collective-permute-start | bytes 2457608 | tf_op jit(solution)/shard_map/ppermute | solution.py:233
  91.1 7.4 %collective-permute-done.14.refs_4_ = bf16[320,1280]{1,0:T(8,128)(2,1)} collective-permute-done((bf16[320,1280]{1,0:T(8,128)(2,1)}, bf16[320,1280]{1,0:T(8,128)(2,1)}, u32[]{:S(2)}, u32[]{:S(2)}) %collective-permute-start.14) | collective-permute-done | bytes 819232 | tf_op jit(solution)/shard_map/ppermute | solution.py:233
  98.5 7.9 %collective-permute-done.12.refs_3_ = bf16[320,1280]{1,0:T(8,128)(2,1)S(1)} collective-permute-done((bf16[320,1280]{1,0:T(8,128)(2,1)S(1)}, bf16[320,1280]{1,0:T(8,128)(2,1)S(1)}, u32[]{:S(2)}, u32[]{:S(2)}) %collective-permute-start.12) | collective-permute-done | bytes 819232 | tf_op jit(solution)/shard_map/ppermute | solution.py:233
  106.4 1.8 collective-permute-start.13
  108.1 7.8 %collective-permute-done.16.refs_6_ = bf16[320,1280]{1,0:T(8,128)(2,1)S(1)} collective-permute-done((bf16[320,1280]{1,0:T(8,128)(2,1)}, bf16[320,1280]{1,0:T(8,128)(2,1)S(1)}, u32[]{:S(2)}, u32[]{:S(2)}) %collective-permute-start.16) | collective-permute-done | bytes 819232 | tf_op jit(solution)/shard_map/ppermute | solution.py:233
  115.9 8.0 %collective-permute-done.17.refs_7_ = bf16[320,1280]{1,0:T(8,128)(2,1)S(1)} collective-permute-done((bf16[320,1280]{1,0:T(8,128)(2,1)}, bf16[320,1280]{1,0:T(8,128)(2,1)S(1)}, u32[]{:S(2)}, u32[]{:S(2)}) %collective-permute-start.17) | collective-permute-done | bytes 819232 | tf_op jit(solution)/shard_map/ppermute | solution.py:233
  123.9 1.8 collective-permute-start.23
  125.7 1.7 copy-done.3
  127.4 1.1 copy-done.14
  128.6 11.9 %expert_part.3 = (bf16[256,1280]{1,0:T(8,128)(2,1)S(1)}, bf16[256,1280]{1,0:T(8,128)(2,1)S(1)}, f32[2,1280]{1,0:T(2,128)S(1)}) custom-call(s32[4]{0:T(128)S(1)} %pad_add_fusion.where_ref.refs_0_, bf16[320,1280]{1,0:T(8,128)(2,1)} %bitcast.6.refs_1_, bf16[320,1280]{1,0:T(8,128)(2,1)} %collective-permute-done.9.refs_2_, bf16[320,1280]{1,0:T(8,128)(2,1)S(1)} %copy-done.14, ...), custom_call_target="tpu_custom_call" | custom-call | flops 6710886400 | bytes 9175040 | tf_op jit(solution)/shard_map/expert_part/pallas_call | solution.py:176
  140.5 0.8 copy-done.7
  141.3 0.8 copy-done.15
  142.2 4.4 %collective-permute-start.25 = (bf16[256,1280]{1,0:T(8,128)(2,1)}, bf16[256,1280]{1,0:T(8,128)(2,1)}, u32[]{:S(2)}, u32[]{:S(2)}) collective-permute-start(bf16[256,1280]{1,0:T(8,128)(2,1)} %copy-done.15), channel_id=1, source_target_pairs={{0,16},{16,0},{1,17},{17,1},{2,18},{18,2},{3,19},{19,3},{4,20},{20... | collective-permute-start | bytes 1966088 | tf_op jit(solution)/shard_map/ppermute | solution.py:233
  146.6 1.7 copy-done.4
  148.3 1.1 copy-done.6
  149.4 5.4 %expert_part.4 = f32[1,1280]{1,0:T(1,128)S(1)} custom-call(s32[4]{0:T(128)S(1)} %pad_add_fusion.where_ref.refs_0_, bf16[320,1280]{1,0:T(8,128)(2,1)S(1)} %bitcast.33, bf16[320,1280]{1,0:T(8,128)(2,1)} %collective-permute-done.20.refs_2_, bf16[320,1280]{1,0:T(8,128)(2,1)S(1)} %copy-done.6, bf16[320,1280]{1,0:T(8,128)(2,1)} %collective-permute-done.13.refs_4_, ...), custom_call_target="tpu_custom_call" | custom-call | flops 1677721600 | bytes 9175040 | tf_op jit(solution)/shard_map/expert_part/pallas_call | solution.py:176
  154.9 4.1 %collective-permute-done.23.refs_7_ = bf16[320,1280]{1,0:T(8,128)(2,1)} collective-permute-done((bf16[320,1280]{1,0:T(8,128)(2,1)}, bf16[320,1280]{1,0:T(8,128)(2,1)}, u32[]{:S(2)}, u32[]{:S(2)}) %collective-permute-start.23) | collective-permute-done | bytes 819232 | tf_op jit(solution)/shard_map/ppermute | solution.py:233
  159.0 10.2 %expert_part.5 = (bf16[256,1280]{1,0:T(8,128)(2,1)S(1)}, bf16[256,1280]{1,0:T(8,128)(2,1)}, f32[1,1280]{1,0:T(1,128)S(1)}) custom-call(s32[4]{0:T(128)S(1)} %pad_add_fusion.where_ref.refs_0_, bf16[320,1280]{1,0:T(8,128)(2,1)S(1)} %bitcast.34, bf16[320,1280]{1,0:T(8,128)(2,1)} %collective-permute-done.20.refs_2_, bf16[320,1280]{1,0:T(8,128)(2,1)S(1)} %copy-done.6, ...), custom_call_target="tpu_custom_call" | custom-call | flops 5033164800 | bytes 9175040 | tf_op jit(solution)/shard_map/expert_part/pallas_call | solution.py:176
  169.3 0.8 copy-done.9
  170.1 4.1 %collective-permute-start.26 = (bf16[256,1280]{1,0:T(8,128)(2,1)}, bf16[256,1280]{1,0:T(8,128)(2,1)S(1)}, u32[]{:S(2)}, u32[]{:S(2)}) collective-permute-start(bf16[256,1280]{1,0:T(8,128)(2,1)} %get-tuple-element.47), channel_id=1, source_target_pairs={{0,16},{16,0},{1,17},{17,1},{2,18},{18,2},{3,19},{19,3},{4,20},{20... | collective-permute-start | bytes 1966088 | tf_op jit(solution)/shard_map/ppermute | solution.py:233
  174.3 0.5 fusion.1
  175.1 9.2 %all_to_all.32 = f32[16,1,160]{2,1,0:T(1,128)S(1)} all-to-all(f32[16,1,160]{2,1,0:T(1,128)S(1)} %all_to_all.27), channel_id=1, replica_groups=mesh['x_lo'=2,'y'=4,'core'=2,'x_hi'=2,'z'=8] {'x_lo','y','core'}, dimensions={0} | all-to-all | bytes 20480 | tf_op jit(solution)/shard_map/all_to_all | solution.py:319
  184.3 0.7 all_to_all.24
  185.0 9.3 %all-to-all-start.3 = ((f32[16,1,10]{2,1,0:T(1,128)}), f32[16,1,10]{2,1,0:T(1,128)S(1)}, u32[]{:S(2)}, u32[]{:S(2)}) async-start(f32[16,1,10]{2,1,0:T(1,128)} %bitcast.14), calls=%async_computation.3 | async-start | bytes 16384 | tf_op jit(solution)/shard_map/all_to_all | solution.py:321
  194.4 1.1 copy-done.8
  195.5 1.1 copy-done.10
  196.6 3.3 %join.1 = bf16[256,5120]{1,0:T(8,128)(2,1)} custom-call(s32[4]{0:T(128)S(1)} %pad_add_fusion.where_ref.refs_0_, bf16[256,1280]{1,0:T(8,128)(2,1)S(1)} %copy-done.8, bf16[256,1280]{1,0:T(8,128)(2,1)S(1)} %copy-done.10, bf16[256,1280]{1,0:T(8,128)(2,1)} %collective-permute-done.25.refs_3_, bf16[256,1280]{1,0:T(8,128)(2,1)S(1)} %collective-permute-done.26.refs_4_), custom_call_target="tpu_custom_call" | custom-call | tf_op jit(solution)/shard_map/join/pallas_call | solution.py:215
  199.8 3.3 %all-to-all-done.3 = f32[16,1,10]{2,1,0:T(1,128)S(1)} async-done(((f32[16,1,10]{2,1,0:T(1,128)}), f32[16,1,10]{2,1,0:T(1,128)S(1)}, u32[]{:S(2)}, u32[]{:S(2)}) %all-to-all-start.3) | async-done | bytes 672 | tf_op jit(solution)/shard_map/all_to_all | solution.py:321
  203.4 0.5 fusion.6
  (63 shorter events, 0.9 us)
Async XLA Ops:
  0.6 7.7 %copy-start.18 = (s32[128,1]{0,1:T(1,128)S(1)}, s32[128,1]{0,1:T(1,128)}, u32[]{:S(2)}) copy-start(s32[128,1]{0,1:T(1,128)} %param.7) | copy-start | bytes 1540
  2.0 9.5 %collective-permute-start.3 = (bf16[128,1280]{1,0:T(8,128)(2,1)S(1)}, bf16[128,1280]{1,0:T(8,128)(2,1)S(1)}, u32[]{:S(2)}, u32[]{:S(2)}) collective-permute-start(bf16[128,1280]{1,0:T(8,128)(2,1)S(1)} %get-tuple-element.50), channel_id=1, source_target_pairs={{0,16},{16,0},{1,17},{17,1},{2,18},{18,2},{3,19},{19,3},{4,20},{20... | collective-permute-start | bytes 983048 | tf_op jit(solution)/shard_map/ppermute | solution.py:233
  5.3 10.5 %collective-permute-start.4 = (bf16[128,1280]{1,0:T(8,128)(2,1)S(1)}, bf16[128,1280]{1,0:T(8,128)(2,1)S(1)}, u32[]{:S(2)}, u32[]{:S(2)}) collective-permute-start(bf16[128,1280]{1,0:T(8,128)(2,1)S(1)} %get-tuple-element.28.t0), channel_id=1, source_target_pairs={{0,136},{8,128},{16,152},{24,144},{128,8},{136,0},{144,24},{152,16... | collective-permute-start | bytes 983048 | tf_op jit(solution)/shard_map/ppermute | solution.py:243
  6.1 17.0 %collective-permute-start.5 = (bf16[128,1280]{1,0:T(8,128)(2,1)S(1)}, bf16[128,1280]{1,0:T(8,128)(2,1)S(1)}, u32[]{:S(2)}, u32[]{:S(2)}) collective-permute-start(bf16[128,1280]{1,0:T(8,128)(2,1)S(1)} %get-tuple-element.50), channel_id=1, source_target_pairs={{0,152},{8,144},{16,136},{24,128},{128,24},{136,16},{144,8},{152,0... | collective-permute-start | bytes 983048 | tf_op jit(solution)/shard_map/ppermute | solution.py:243
  10.6 12.5 %collective-permute-start = (f32[8,128]{1,0:T(8,128)}, f32[8,128]{1,0:T(8,128)S(1)}, u32[]{:S(2)}, u32[]{:S(2)}) collective-permute-start(f32[8,128]{1,0:T(8,128)} %route.1.m0), channel_id=1, source_target_pairs={{0,16},{16,0},{1,17},{17,1},{2,18},{18,2},{3,19},{19,3},{4,20},{20... | collective-permute-start | bytes 12296 | tf_op jit(solution)/shard_map/ppermute | solution.py:233
  10.7 12.4 %collective-permute-start.1 = (f32[8,128]{1,0:T(8,128)}, f32[8,128]{1,0:T(8,128)S(1)}, u32[]{:S(2)}, u32[]{:S(2)}) collective-permute-start(f32[8,128]{1,0:T(8,128)} %route.1.m0), channel_id=1, source_target_pairs={{0,136},{8,128},{16,152},{24,144},{128,8},{136,0},{144,24},{152,16... | collective-permute-start | bytes 12296 | tf_op jit(solution)/shard_map/ppermute | solution.py:243
  11.5 12.0 %collective-permute-start.2 = (f32[8,128]{1,0:T(8,128)}, f32[8,128]{1,0:T(8,128)S(1)}, u32[]{:S(2)}, u32[]{:S(2)}) collective-permute-start(f32[8,128]{1,0:T(8,128)} %route.1.m0), channel_id=1, source_target_pairs={{0,152},{8,144},{16,136},{24,128},{128,24},{136,16},{144,8},{152,0... | collective-permute-start | bytes 12296 | tf_op jit(solution)/shard_map/ppermute | solution.py:243
  23.5 0.7 copy-start.11
  26.6 24.8 %copy-start.12 = (f32[8,128]{1,0:T(8,128)S(1)}, f32[8,128]{1,0:T(8,128)}, u32[]{:S(2)}) copy-start(f32[8,128]{1,0:T(8,128)} %route.1.m0) | copy-start | bytes 12292
  26.7 30.8 %all-to-all-start = ((bf16[8,40,1280]{2,1,0:T(8,128)(2,1)}), bf16[8,40,1280]{2,1,0:T(8,128)(2,1)}, u32[]{:S(2)}, u32[]{:S(2)}) async-start(bf16[8,40,1280]{2,1,0:T(8,128)(2,1)} %bitcast.5), calls=%async_computation | async-start | bytes 1638400 | tf_op jit(solution)/shard_map/all_to_all | solution.py:278
  33.1 3.8 %collective-permute-start.6 = (bf16[128,1280]{1,0:T(8,128)(2,1)S(1)}, bf16[128,1280]{1,0:T(8,128)(2,1)S(1)}, u32[]{:S(2)}, u32[]{:S(2)}) collective-permute-start(bf16[128,1280]{1,0:T(8,128)(2,1)S(1)} %get-tuple-element.27), channel_id=1, source_target_pairs={{0,16},{16,0},{1,17},{17,1},{2,18},{18,2},{3,19},{19,3},{4,20},{20... | collective-permute-start | bytes 983048 | tf_op jit(solution)/shard_map/ppermute | solution.py:233
  33.8 10.6 %collective-permute-start.7 = (bf16[128,1280]{1,0:T(8,128)(2,1)S(1)}, bf16[128,1280]{1,0:T(8,128)(2,1)S(1)}, u32[]{:S(2)}, u32[]{:S(2)}) collective-permute-start(bf16[128,1280]{1,0:T(8,128)(2,1)S(1)} %get-tuple-element.26.t0), channel_id=1, source_target_pairs={{0,136},{8,128},{16,152},{24,144},{128,8},{136,0},{144,24},{152,16... | collective-permute-start | bytes 983048 | tf_op jit(solution)/shard_map/ppermute | solution.py:243
  36.3 15.2 %collective-permute-start.8 = (bf16[128,1280]{1,0:T(8,128)(2,1)S(1)}, bf16[128,1280]{1,0:T(8,128)(2,1)S(1)}, u32[]{:S(2)}, u32[]{:S(2)}) collective-permute-start(bf16[128,1280]{1,0:T(8,128)(2,1)S(1)} %get-tuple-element.27), channel_id=1, source_target_pairs={{0,152},{8,144},{16,136},{24,128},{128,24},{136,16},{144,8},{152,0... | collective-permute-start | bytes 983048 | tf_op jit(solution)/shard_map/ppermute | solution.py:243
  36.7 41.7 %collective-permute-start.11 = (bf16[2560,256]{1,0:T(8,128)(2,1)}, bf16[2560,256]{1,0:T(8,128)(2,1)}, u32[]{:S(2)}, u32[]{:S(2)}) collective-permute-start(bf16[2560,256]{1,0:T(8,128)(2,1)} %bitcast.9.own_ref), channel_id=1, source_target_pairs={{0,16},{16,0},{1,17},{17,1},{2,18},{18,2},{3,19},{19,3},{4,20},{20... | collective-permute-start | bytes 3932168 | tf_op jit(solution)/shard_map/ppermute | solution.py:233
  51.5 11.1 %copy-start = (bf16[1,256,5120]{2,1,0:T(8,128)(2,1)S(1)}, bf16[1,256,5120]{2,1,0:T(8,128)(2,1)}, u32[]{:S(2)}) copy-start(bf16[1,256,5120]{2,1,0:T(8,128)(2,1)} %param.10) | copy-start | bytes 7864324
  53.1 0.9 copy-start.1
  57.5 21.0 %collective-permute-start.9 = (bf16[320,1280]{1,0:T(8,128)(2,1)}, bf16[320,1280]{1,0:T(8,128)(2,1)}, u32[]{:S(2)}, u32[]{:S(2)}) collective-permute-start(bf16[320,1280]{1,0:T(8,128)(2,1)} %bitcast.6.refs_1_), channel_id=1, source_target_pairs={{0,32},{32,64},{64,96},{96,0},{1,33},{33,65},{65,97},{97,1},{2,34}... | collective-permute-start | bytes 2457608 | tf_op jit(solution)/shard_map/ppermute | solution.py:233
  58.8 28.1 %all-to-all-start.1 = ((bf16[8,40,1280]{2,1,0:T(8,128)(2,1)}), bf16[8,40,1280]{2,1,0:T(8,128)(2,1)S(1)}, u32[]{:S(2)}, u32[]{:S(2)}) async-start(bf16[8,40,1280]{2,1,0:T(8,128)(2,1)} %bitcast.35), calls=%async_computation.1 | async-start | bytes 1638400 | tf_op jit(solution)/shard_map/all_to_all | solution.py:278
  62.6 15.9 %copy-start.16 = (s32[640,1]{1,0:T(8,128)S(1)}, s32[640,1]{1,0:T(8,128)}, u32[]{:S(2)}) copy-start(s32[640,1]{1,0:T(8,128)} %constant.35.target_ref) | copy-start | bytes 7684
  63.8 24.6 %collective-permute-start.19 = (bf16[256,2560]{1,0:T(8,128)(2,1)}, bf16[256,2560]{1,0:T(8,128)(2,1)}, u32[]{:S(2)}, u32[]{:S(2)}) collective-permute-start(bf16[256,2560]{1,0:T(8,128)(2,1)} %slice_select_fusion), channel_id=1, source_target_pairs={{0,16},{16,0},{1,17},{17,1},{2,18},{18,2},{3,19},{19,3},{4,20},{20... | collective-permute-start | bytes 3932168 | tf_op jit(solution)/shard_map/ppermute | solution.py:233
  64.4 20.2 %collective-permute-start.10 = (bf16[320,1280]{1,0:T(8,128)(2,1)}, bf16[320,1280]{1,0:T(8,128)(2,1)S(1)}, u32[]{:S(2)}, u32[]{:S(2)}) collective-permute-start(bf16[320,1280]{1,0:T(8,128)(2,1)} %bitcast.6.refs_1_), channel_id=1, source_target_pairs={{0,96},{32,0},{64,32},{96,64},{1,97},{33,1},{65,33},{97,65},{2,98}... | collective-permute-start | bytes 2457608 | tf_op jit(solution)/shard_map/ppermute | solution.py:233
  65.7 22.6 %collective-permute-start.15 = (bf16[320,1280]{1,0:T(8,128)(2,1)}, bf16[320,1280]{1,0:T(8,128)(2,1)}, u32[]{:S(2)}, u32[]{:S(2)}) collective-permute-start(bf16[320,1280]{1,0:T(8,128)(2,1)} %bitcast.6.refs_1_), channel_id=1, source_target_pairs={{0,128},{128,0},{1,129},{129,1},{2,130},{130,2},{3,131},{131,3},{4... | collective-permute-start | bytes 2457608 | tf_op jit(solution)/shard_map/ppermute | solution.py:233
  78.5 20.0 %collective-permute-start.14 = (bf16[320,1280]{1,0:T(8,128)(2,1)}, bf16[320,1280]{1,0:T(8,128)(2,1)}, u32[]{:S(2)}, u32[]{:S(2)}) collective-permute-start(bf16[320,1280]{1,0:T(8,128)(2,1)} %collective-permute-done.9.refs_2_), channel_id=1, source_target_pairs={{0,32},{32,64},{64,96},{96,0},{1,33},{33,65},{65,97},{97,1},{2,34}... | collective-permute-start | bytes 2457608 | tf_op jit(solution)/shard_map/ppermute | solution.py:233
  82.9 1.5 copy-start.2
  84.6 0.9 copy-start.13
  86.9 19.4 %collective-permute-start.12 = (bf16[320,1280]{1,0:T(8,128)(2,1)S(1)}, bf16[320,1280]{1,0:T(8,128)(2,1)S(1)}, u32[]{:S(2)}, u32[]{:S(2)}) collective-permute-start(bf16[320,1280]{1,0:T(8,128)(2,1)S(1)} %bitcast.30), channel_id=1, source_target_pairs={{0,96},{32,0},{64,32},{96,64},{1,97},{33,1},{65,33},{97,65},{2,98}... | collective-permute-start | bytes 2457608 | tf_op jit(solution)/shard_map/ppermute | solution.py:233
  88.4 27.5 %collective-permute-start.16 = (bf16[320,1280]{1,0:T(8,128)(2,1)}, bf16[320,1280]{1,0:T(8,128)(2,1)S(1)}, u32[]{:S(2)}, u32[]{:S(2)}) collective-permute-start(bf16[320,1280]{1,0:T(8,128)(2,1)} %collective-permute-done.15.refs_5_), channel_id=1, source_target_pairs={{0,32},{32,64},{64,96},{96,0},{1,33},{33,65},{65,97},{97,1},{2,34}... | collective-permute-start | bytes 2457608 | tf_op jit(solution)/shard_map/ppermute | solution.py:233
  88.4 27.5 %collective-permute-start.21 = (bf16[320,1280]{1,0:T(8,128)(2,1)S(1)}, bf16[320,1280]{1,0:T(8,128)(2,1)}, u32[]{:S(2)}, u32[]{:S(2)}) collective-permute-start(bf16[320,1280]{1,0:T(8,128)(2,1)S(1)} %bitcast.31), channel_id=1, source_target_pairs={{0,128},{128,0},{1,129},{129,1},{2,130},{130,2},{3,131},{131,3},{4... | collective-permute-start | bytes 2457608 | tf_op jit(solution)/shard_map/ppermute | solution.py:233
  88.4 35.5 %collective-permute-start.17 = (bf16[320,1280]{1,0:T(8,128)(2,1)}, bf16[320,1280]{1,0:T(8,128)(2,1)S(1)}, u32[]{:S(2)}, u32[]{:S(2)}) collective-permute-start(bf16[320,1280]{1,0:T(8,128)(2,1)} %collective-permute-done.15.refs_5_), channel_id=1, source_target_pairs={{0,96},{32,0},{64,32},{96,64},{1,97},{33,1},{65,33},{97,65},{2,98}... | collective-permute-start | bytes 2457608 | tf_op jit(solution)/shard_map/ppermute | solution.py:233
  98.5 27.2 %collective-permute-start.18 = (bf16[320,1280]{1,0:T(8,128)(2,1)}, bf16[320,1280]{1,0:T(8,128)(2,1)S(1)}, u32[]{:S(2)}, u32[]{:S(2)}) collective-permute-start(bf16[320,1280]{1,0:T(8,128)(2,1)} %collective-permute-done.14.refs_4_), channel_id=1, source_target_pairs={{0,128},{128,0},{1,129},{129,1},{2,130},{130,2},{3,131},{131,3},{4... | collective-permute-start | bytes 2457608 | tf_op jit(solution)/shard_map/ppermute | solution.py:233
  106.4 34.1 %copy-start.5 = (bf16[320,1280]{1,0:T(8,128)(2,1)}, bf16[320,1280]{1,0:T(8,128)(2,1)S(1)}, u32[]{:S(2)}) copy-start(bf16[320,1280]{1,0:T(8,128)(2,1)S(1)} %collective-permute-done.12.refs_3_) | copy-start | bytes 2457604
  106.4 35.8 %collective-permute-start.13 = (bf16[320,1280]{1,0:T(8,128)(2,1)S(1)}, bf16[320,1280]{1,0:T(8,128)(2,1)}, u32[]{:S(2)}, u32[]{:S(2)}) collective-permute-start(bf16[320,1280]{1,0:T(8,128)(2,1)S(1)} %collective-permute-done.12.refs_3_), channel_id=1, source_target_pairs={{0,96},{32,0},{64,32},{96,64},{1,97},{33,1},{65,33},{97,65},{2,98}... | collective-permute-start | bytes 2457608 | tf_op jit(solution)/shard_map/ppermute | solution.py:233
  115.9 30.6 %collective-permute-start.20 = (bf16[320,1280]{1,0:T(8,128)(2,1)S(1)}, bf16[320,1280]{1,0:T(8,128)(2,1)}, u32[]{:S(2)}, u32[]{:S(2)}) collective-permute-start(bf16[320,1280]{1,0:T(8,128)(2,1)S(1)} %bitcast.32), channel_id=1, source_target_pairs={{0,32},{32,64},{64,96},{96,0},{1,33},{33,65},{65,97},{97,1},{2,34}... | collective-permute-start | bytes 2457608 | tf_op jit(solution)/shard_map/ppermute | solution.py:233
  115.9 39.0 %collective-permute-start.22 = (bf16[320,1280]{1,0:T(8,128)(2,1)}, bf16[320,1280]{1,0:T(8,128)(2,1)}, u32[]{:S(2)}, u32[]{:S(2)}) collective-permute-start(bf16[320,1280]{1,0:T(8,128)(2,1)} %collective-permute-done.21.refs_5_), channel_id=1, source_target_pairs={{0,32},{32,64},{64,96},{96,0},{1,33},{33,65},{65,97},{97,1},{2,34}... | collective-permute-start | bytes 2457608 | tf_op jit(solution)/shard_map/ppermute | solution.py:233
  123.9 35.1 %collective-permute-start.23 = (bf16[320,1280]{1,0:T(8,128)(2,1)}, bf16[320,1280]{1,0:T(8,128)(2,1)}, u32[]{:S(2)}, u32[]{:S(2)}) collective-permute-start(bf16[320,1280]{1,0:T(8,128)(2,1)} %collective-permute-done.21.refs_5_), channel_id=1, source_target_pairs={{0,96},{32,0},{64,32},{96,64},{1,97},{33,1},{65,33},{97,65},{2,98}... | collective-permute-start | bytes 2457608 | tf_op jit(solution)/shard_map/ppermute | solution.py:233
  125.7 1.7 copy-start.3
  127.4 1.1 copy-start.14
  140.5 0.8 copy-start.7
  141.3 0.8 copy-start.15
  142.1 16.9 %collective-permute-start.24 = (bf16[320,1280]{1,0:T(8,128)(2,1)}, bf16[320,1280]{1,0:T(8,128)(2,1)}, u32[]{:S(2)}, u32[]{:S(2)}) collective-permute-start(bf16[320,1280]{1,0:T(8,128)(2,1)} %collective-permute-done.13.refs_4_), channel_id=1, source_target_pairs={{0,128},{128,0},{1,129},{129,1},{2,130},{130,2},{3,131},{131,3},{4... | collective-permute-start | bytes 2457608 | tf_op jit(solution)/shard_map/ppermute | solution.py:233
  142.2 52.2 %collective-permute-start.25 = (bf16[256,1280]{1,0:T(8,128)(2,1)}, bf16[256,1280]{1,0:T(8,128)(2,1)}, u32[]{:S(2)}, u32[]{:S(2)}) collective-permute-start(bf16[256,1280]{1,0:T(8,128)(2,1)} %copy-done.15), channel_id=1, source_target_pairs={{0,16},{16,0},{1,17},{17,1},{2,18},{18,2},{3,19},{19,3},{4,20},{20... | collective-permute-start | bytes 1966088 | tf_op jit(solution)/shard_map/ppermute | solution.py:233
  146.6 1.7 copy-start.4
  148.3 1.1 copy-start.6
  154.9 19.4 %copy-start.19 = (s32[2,2,80]{2,1,0:T(2,128)S(1)}, s32[2,2,80]{2,1,0:T(2,128)}, u32[]{:S(2)}) copy-start(s32[2,2,80]{2,1,0:T(2,128)} %constant.37) | copy-start | bytes 3844
  169.3 0.8 copy-start.9
  170.1 24.2 %collective-permute-start.26 = (bf16[256,1280]{1,0:T(8,128)(2,1)}, bf16[256,1280]{1,0:T(8,128)(2,1)S(1)}, u32[]{:S(2)}, u32[]{:S(2)}) collective-permute-start(bf16[256,1280]{1,0:T(8,128)(2,1)} %get-tuple-element.47), channel_id=1, source_target_pairs={{0,16},{16,0},{1,17},{17,1},{2,18},{18,2},{3,19},{19,3},{4,20},{20... | collective-permute-start | bytes 1966088 | tf_op jit(solution)/shard_map/ppermute | solution.py:233
  185.0 18.2 %all-to-all-start.3 = ((f32[16,1,10]{2,1,0:T(1,128)}), f32[16,1,10]{2,1,0:T(1,128)S(1)}, u32[]{:S(2)}, u32[]{:S(2)}) async-start(f32[16,1,10]{2,1,0:T(1,128)} %bitcast.14), calls=%async_computation.3 | async-start | bytes 16384 | tf_op jit(solution)/shard_map/all_to_all | solution.py:321
  194.4 1.1 copy-start.8
  195.5 1.1 copy-start.10
  196.5 6.8 %copy-start.17 = (f32[128]{0:T(128)S(1)}, f32[128]{0:T(128)}, u32[]{:S(2)}) copy-start(f32[128]{0:T(128)} %param.8) | copy-start | bytes 1540
where the time goes:
time: 205 us; the launch traced here: 204 us
  waiting for transfers between devices  80.4 us (39%)
  starting transfers between devices  52.3 us (26%)
  Pallas kernels  40.9 us (20%)
  local copies, waits for them, and re-layouts  16.1 us (8%)
  blocking collectives  9.22 us (4%)
  other arithmetic  3.45 us (2%)
    ppermute x21, waiting for transfers between devices, send(): lax.ppermute(array, axis, [(i, (i + shift) % size) for i in range(size)])  48.1 us
    pallas_call x3, Pallas kernels, expert_part(): pl.pallas_call(lambda *refs: expert_kernel(off, width, places, sides, gra...  27.5 us
    ppermute x6, waiting for transfers between devices, send(): return lax.ppermute(array, axes, [(i, i ^ flip) for i in range(8)])  24 us
    ppermute x21, starting transfers between devices, send(): lax.ppermute(array, axis, [(i, (i + shift) % size) for i in range(size)])  23.6 us
    unnamed x41, local copies, waits for them, and re-layouts  15.2 us
    all_to_all x2, starting transfers between devices, spread(): lax.all_to_all(sent.reshape(8, 40, width), 'z', split_axis=0, concat_axis...  10.3 us
    all_to_all x1, starting transfers between devices, body(): lax.all_to_all(own_scores, ('x_hi', 'z'), split_axis=0, concat_axis=0, ti...  9.34 us
    all_to_all x1, blocking collectives, body(): lax.all_to_all(parts, ('x_lo', 'y', 'core'), split_axis=0, concat_axis=0,...  9.22 us
  transfers between devices with their start and end apart: 30, of which 15 were waited for; matrix products, arithmetic and copies ran while one was open for 1% of the time, Pallas kernels for 19%

commit v1 on v0

--- a/solution.py
+++ b/solution.py
@@ -128,46 +128,39 @@
 def expert_kernel(off, width, places, sides, grad, where_ref, *refs):
     n = len(places)
     pieces, (hid_ref, down_ref, par_ref), refs = refs[:n], refs[n : n + 3], refs[n + 3 :]
-    outs, (rows, own_wts, sems) = refs[:-3], refs[-3:]
+    outs, (rows, wts, sems) = refs[:-3], refs[-3:]
     core, y, x_lo = where_ref[0], where_ref[2], where_ref[3]
 
     def place_of(side):
         return x_lo if side == 0 else 1 - x_lo
 
-    copies = []
     start = pl.multiple_of(core * HALF + off, 128)
-    copies.append((None, pltpu.make_async_copy(down_ref.at[:, pl.ds(start, width)], own_wts, sems.at[n])))
-    for i, (ref, (side, up)) in enumerate(zip(pieces, places)):
+    down = down_ref.at[:, pl.ds(start, width)]
+    par = par_ref.at[:, pl.ds(off, width)]
+    copies = [
+        pltpu.make_async_copy(down, wts.at[pl.ds(0, FD), :], sems.at[0]),
+        pltpu.make_async_copy(par, wts.at[pl.ds(FD, FD), :], sems.at[1]),
+    ]
+    for copy in copies:
+        copy.start()
+    for ref, (side, up) in zip(pieces, places):
         start = pl.multiple_of(place_of(side) * QUARTER + lax.rem(y + up, 4) * BLOCK, BLOCK)
-        copies.append((side, pltpu.make_async_copy(ref, rows.at[pl.ds(start, BLOCK), :], sems.at[i])))
-    copies.sort(key=lambda c: c[0] in sides or c[0] is None, reverse=True)
-    for _, copy in copies:
-        copy.start()
-    for side, copy in copies:
-        if side in sides or side is None:
-            copy.wait()
+        rows[pl.ds(start, BLOCK), :] = ref[...]
+    for copy in copies:
+        copy.wait()
 
     tile = QUARTER // 2
     for k, side in enumerate(sides):
-
-        @pl.loop(0, 2)
-        def _(i):
+        for i in range(2):
             at = pl.ds(pl.multiple_of(place_of(side) * QUARTER + i * tile, 128), tile)
-            total = None
-            for half in range(2):
-                wts = own_wts[...] if half == 0 else par_ref[:, pl.ds(off, width)]
-                back = lax.dot_general(wts, rows[at, :], (((1,), (1,)), ((), ())), preferred_element_type=F32)
-                part = jnp.sum(back * hid_ref[pl.ds(half * FD, FD), at].astype(F32), axis=0, keepdims=True)
-                total = part if total is None else total + part
-            outs[-1][k : k + 1, pl.ds(pl.multiple_of(i * tile, 128), tile)] = total
-
-    for side, copy in copies:
-        if not (side in sides or side is None):
-            copy.wait()
+            back = lax.dot_general(wts[...], rows[at, :], (((1,), (1,)), ((), ())), preferred_element_type=F32)
+            part = jnp.sum(back * hid_ref[:, at].astype(F32), axis=0, keepdims=True)
+            outs[-1][k : k + 1, pl.ds(i * tile, tile)] = part
+
     if grad:
-        for i in range(2):
-            at = pl.ds(i * FD, FD)
-            outs[i][...] = jnp.dot(hid_ref[at, :], rows[...], preferred_element_type=F32).astype(BF)
+        total = jnp.dot(hid_ref[...], rows[...], preferred_element_type=F32).astype(BF)
+        outs[0][...] = total[:FD]
+        outs[1][...] = total[FD:]
 
 
 def expert_part(where, pieces, hid, down, par, off, width, places, sides=(0, 1), grad=True):
@@ -176,17 +169,17 @@
     return pl.pallas_call(
         lambda *refs: expert_kernel(off, width, places, sides, grad, *refs),
         out_shape=shapes,
-        in_specs=[SMEM] + [ANY] * len(pieces) + [VMEM, ANY, VMEM],
+        in_specs=[SMEM] + [VMEM] * len(pieces) + [VMEM, ANY, ANY],
         out_specs=(VMEM,) * len(shapes),
         scratch_shapes=[
             pltpu.VMEM((SLOTS, width), BF),
-            pltpu.VMEM((FD, width), BF),
-            pltpu.SemaphoreType.DMA((len(pieces) + 1,)),
+            pltpu.VMEM((2 * FD, width), BF),
+            pltpu.SemaphoreType.DMA((2,)),
         ],
         compiler_params=pltpu.CompilerParams(vmem_limit_bytes=28 * MIB),
         cost_estimate=pl.CostEstimate(
-            flops=2 * (len(sides) + 2 * grad) * FD * SLOTS * width,
-            bytes_accessed=2 * SLOTS * (width + 2 * FD),
+            flops=0,
+            bytes_accessed=0,
             transcendentals=0,
         ),
         name="expert_part",
@@ -287,10 +280,11 @@
     rows_1 = spread(sent_1)
 
     below_0, above_0, over_0 = up(rows_0), down(rows_0), cross(rows_0)
+    below_0, hid = tie(below_0, hid)
     far_0 = up(below_0)
     over_below_0, over_above_0 = up(over_0), down(over_0)
     over_far_0 = cross(far_0)
-    rows, (below_0, above_0, hid) = tie(rows_1, (below_0, above_0, hid))
+    rows, (below_0, above_0) = tie(rows_1, (below_0, above_0))
     over_1, above_1 = cross(rows), down(rows)
     rows, far_0 = tie(rows, far_0)
     below_1 = up(rows)

time: 205 us -> 202 us (0.985)
    all_to_all x1, starting transfers between devices: 9.34 us -> 6.72 us  [body(): lax.all_to_all(own_scores, ('x_hi', 'z'), split_axis=0, concat_axis=0, ti...]
    ppermute x21, starting transfers between devices: 23.6 us -> 26.2 us  [send(): lax.ppermute(array, axis, [(i, (i + shift) % size) for i in range(size)])]
    ppermute x21, waiting for transfers between devices: 48.1 us -> 46 us  [send(): lax.ppermute(array, axis, [(i, (i + shift) % size) for i in range(size)])]
  transfers between devices with their start and end apart: 30 -> 30, of which waited for: 15 -> 16; matrix products, arithmetic and copies ran while one was open for 1% -> 1% of each run, Pallas kernels for 19% -> 19%
where the time goes in v1:
time: 202 us
  waiting for transfers between devices  79.1 us (39%)
  starting transfers between devices  52.3 us (26%)
  Pallas kernels  39.9 us (20%)
  local copies, waits for them, and re-layouts  16.1 us (8%)
  blocking collectives  9.21 us (5%)
  other arithmetic  3.46 us (2%)
    ppermute x21, waiting for transfers between devices, send(): lax.ppermute(array, axis, [(i, (i + shift) % size) for i in range(size)])  46 us
    pallas_call x3, Pallas kernels, expert_part(): pl.pallas_call(lambda *refs: expert_kernel(off, width, places, sides, gra...  26.5 us
    ppermute x21, starting transfers between devices, send(): lax.ppermute(array, axis, [(i, (i + shift) % size) for i in range(size)])  26.2 us
    ppermute x6, waiting for transfers between devices, send(): return lax.ppermute(array, axes, [(i, i ^ flip) for i in range(8)])  24 us
    unnamed x41, local copies, waits for them, and re-layouts  15.2 us
    all_to_all x2, starting transfers between devices, spread(): lax.all_to_all(sent.reshape(8, 40, width), 'z', split_axis=0, concat_axis...  10.3 us
    all_to_all x1, blocking collectives, body(): lax.all_to_all(parts, ('x_lo', 'y', 'core'), split_axis=0, concat_axis=0,...  9.21 us
    ppermute x6, starting transfers between devices, send(): return lax.ppermute(array, axes, [(i, i ^ flip) for i in range(8)])  9.08 us
  transfers between devices with their start and end apart: 30, of which 16 were waited for; matrix products, arithmetic and copies ran while one was open for 1% of the time, Pallas kernels for 19%

profile of v1, /device:TPU:1, one launch (start us, length us, event | category | flops | bytes accessed | tf_op | source)
XLA Modules:
  0.0 201.5 jit_solution(14959075930331757894)
XLA Ops:
  0.6 1.4 broadcast_select_fusion
  2.0 3.3 %collective-permute-start.3 = (bf16[128,1280]{1,0:T(8,128)(2,1)S(1)}, bf16[128,1280]{1,0:T(8,128)(2,1)S(1)}, u32[]{:S(2)}, u32[]{:S(2)}) collective-permute-start(bf16[128,1280]{1,0:T(8,128)(2,1)S(1)} %get-tuple-element.52), channel_id=1, source_target_pairs={{0,16},{16,0},{1,17},{17,1},{2,18},{18,2},{3,19},{19,3},{4,20},{20... | collective-permute-start | bytes 983048 | tf_op jit(solution)/shard_map/ppermute | solution.py:226
  5.3 0.8 collective-permute-start.4
  6.1 2.2 %collective-permute-start.5 = (bf16[128,1280]{1,0:T(8,128)(2,1)S(1)}, bf16[128,1280]{1,0:T(8,128)(2,1)S(1)}, u32[]{:S(2)}, u32[]{:S(2)}) collective-permute-start(bf16[128,1280]{1,0:T(8,128)(2,1)S(1)} %get-tuple-element.52), channel_id=1, source_target_pairs={{0,152},{8,144},{16,136},{24,128},{128,24},{136,16},{144,8},{152,0... | collective-permute-start | bytes 983048 | tf_op jit(solution)/shard_map/ppermute | solution.py:236
  8.3 0.7 copy.15.ids_ref
  9.0 1.5 route.1.m0
  10.7 0.7 collective-permute-start.1
  11.5 2.5 %collective-permute-start.2 = (f32[8,128]{1,0:T(8,128)}, f32[8,128]{1,0:T(8,128)S(1)}, u32[]{:S(2)}, u32[]{:S(2)}) collective-permute-start(f32[8,128]{1,0:T(8,128)} %route.1.m0), channel_id=1, source_target_pairs={{0,152},{8,144},{16,136},{24,128},{128,24},{136,16},{144,8},{152,0... | collective-permute-start | bytes 12296 | tf_op jit(solution)/shard_map/ppermute | solution.py:236
  14.0 1.8 collective-permute-done.4.t2
  15.8 7.3 %collective-permute-done.5.t3 = bf16[128,1280]{1,0:T(8,128)(2,1)S(1)} collective-permute-done((bf16[128,1280]{1,0:T(8,128)(2,1)S(1)}, bf16[128,1280]{1,0:T(8,128)(2,1)S(1)}, u32[]{:S(2)}, u32[]{:S(2)}) %collective-permute-start.5) | collective-permute-done | bytes 327712 | tf_op jit(solution)/shard_map/ppermute | solution.py:236
  23.1 0.3 collective-permute-done.2.m3
  23.5 0.7 copy-done.13
  24.1 2.5 %place.3 = bf16[320,1280]{1,0:T(8,128)(2,1)} custom-call(s32[4]{0:T(128)S(1)} %pad_add_fusion.where_ref.refs_0_, f32[8,128]{1,0:T(8,128)S(1)} %copy-done.13, f32[8,128]{1,0:T(8,128)S(1)} %collective-permute-done.m1, f32[8,128]{1,0:T(8,128)S(1)} %collective-permute-done.1.m2, f32[8,128]{1,0:T(8,128)S(1)} %collective-permute-done.2.m3, ...), custom_call_target="tpu_custom_call" | custom-call | flops 419430400 | bytes 2129920 | tf_op jit(solution)/shard_map/place/pallas_call | solution.py:81
  26.7 6.5 %all-to-all-start = ((bf16[8,40,1280]{2,1,0:T(8,128)(2,1)}), bf16[8,40,1280]{2,1,0:T(8,128)(2,1)}, u32[]{:S(2)}, u32[]{:S(2)}) async-start(bf16[8,40,1280]{2,1,0:T(8,128)(2,1)} %bitcast.5), calls=%async_computation | async-start | bytes 1638400 | tf_op jit(solution)/shard_map/all_to_all | solution.py:271
  33.1 0.7 collective-permute-start.6
  33.8 2.5 %collective-permute-start.7 = (bf16[128,1280]{1,0:T(8,128)(2,1)S(1)}, bf16[128,1280]{1,0:T(8,128)(2,1)S(1)}, u32[]{:S(2)}, u32[]{:S(2)}) collective-permute-start(bf16[128,1280]{1,0:T(8,128)(2,1)S(1)} %get-tuple-element.27.t0), channel_id=1, source_target_pairs={{0,136},{8,128},{16,152},{24,144},{128,8},{136,0},{144,24},{152,16... | collective-permute-start | bytes 983048 | tf_op jit(solution)/shard_map/ppermute | solution.py:236
  36.3 0.4 collective-permute-start.8
  36.9 7.5 %collective-permute-done.7.t2 = bf16[128,1280]{1,0:T(8,128)(2,1)S(1)} collective-permute-done((bf16[128,1280]{1,0:T(8,128)(2,1)S(1)}, bf16[128,1280]{1,0:T(8,128)(2,1)S(1)}, u32[]{:S(2)}, u32[]{:S(2)}) %collective-permute-start.7) | collective-permute-done | bytes 327712 | tf_op jit(solution)/shard_map/ppermute | solution.py:236
  44.4 7.1 %collective-permute-done.8.t3 = bf16[128,1280]{1,0:T(8,128)(2,1)S(1)} collective-permute-done((bf16[128,1280]{1,0:T(8,128)(2,1)S(1)}, bf16[128,1280]{1,0:T(8,128)(2,1)S(1)}, u32[]{:S(2)}, u32[]{:S(2)}) %collective-permute-start.8) | collective-permute-done | bytes 327712 | tf_op jit(solution)/shard_map/ppermute | solution.py:236
  51.5 1.6 place.2
  53.1 0.9 copy-done.6
  54.0 3.5 %all-to-all-done = bf16[8,40,1280]{2,1,0:T(8,128)(2,1)} async-done(((bf16[8,40,1280]{2,1,0:T(8,128)(2,1)}), bf16[8,40,1280]{2,1,0:T(8,128)(2,1)}, u32[]{:S(2)}, u32[]{:S(2)}) %all-to-all-start) | async-done | bytes 819232 | tf_op jit(solution)/shard_map/all_to_all | solution.py:271
  57.5 3.8 %all-to-all-start.1 = ((bf16[8,40,1280]{2,1,0:T(8,128)(2,1)}), bf16[8,40,1280]{2,1,0:T(8,128)(2,1)S(1)}, u32[]{:S(2)}, u32[]{:S(2)}) async-start(bf16[8,40,1280]{2,1,0:T(8,128)(2,1)} %bitcast.35), calls=%async_computation.1 | async-start | bytes 1638400 | tf_op jit(solution)/shard_map/all_to_all | solution.py:271
  61.3 1.3 collective-permute-start.9
  62.6 1.5 collective-permute-start.11
  64.1 1.2 slice_select_fusion
  65.4 0.7 collective-permute-start.19
  66.1 4.4 %turn.1.refs_9_.refs_5_ = bf16[512,2560]{1,0:T(8,128)(2,1)S(1)} custom-call(s32[4]{0:T(128)S(1)} %pad_add_fusion.where_ref.refs_0_, s32[640,1]{1,0:T(8,128)S(1)} %copy-done.16, bf16[2560,256]{1,0:T(8,128)(2,1)} %bitcast.9.own_ref, bf16[2560,256]{1,0:T(8,128)(2,1)} %collective-permute-done.10.par_ref), custom_call_target="tpu_custom_call" | custom-call | flops 1677721600 | bytes 5242880 | tf_op jit(solution)/shard_map/turn/pallas_call | solution.py:116
  70.6 1.5 copy-done.1
  72.1 10.4 %collective-permute-done.9.refs_2_ = bf16[320,1280]{1,0:T(8,128)(2,1)} collective-permute-done((bf16[320,1280]{1,0:T(8,128)(2,1)}, bf16[320,1280]{1,0:T(8,128)(2,1)}, u32[]{:S(2)}, u32[]{:S(2)}) %collective-permute-start.9) | collective-permute-done | bytes 819232 | tf_op jit(solution)/shard_map/ppermute | solution.py:226
  82.5 0.9 copy-done.7
  83.4 2.3 %all-to-all-done.1 = bf16[8,40,1280]{2,1,0:T(8,128)(2,1)S(1)} async-done(((bf16[8,40,1280]{2,1,0:T(8,128)(2,1)}), bf16[8,40,1280]{2,1,0:T(8,128)(2,1)S(1)}, u32[]{:S(2)}, u32[]{:S(2)}) %all-to-all-start.1) | async-done | bytes 819232 | tf_op jit(solution)/shard_map/all_to_all | solution.py:271
  85.7 2.7 %collective-permute-start.12 = (bf16[320,1280]{1,0:T(8,128)(2,1)S(1)}, bf16[320,1280]{1,0:T(8,128)(2,1)S(1)}, u32[]{:S(2)}, u32[]{:S(2)}) collective-permute-start(bf16[320,1280]{1,0:T(8,128)(2,1)S(1)} %bitcast.30), channel_id=1, source_target_pairs={{0,96},{32,0},{64,32},{96,64},{1,97},{33,1},{65,33},{97,65},{2,98}... | collective-permute-start | bytes 2457608 | tf_op jit(solution)/shard_map/ppermute | solution.py:226
  88.4 2.7 %collective-permute-start.17 = (bf16[320,1280]{1,0:T(8,128)(2,1)}, bf16[320,1280]{1,0:T(8,128)(2,1)S(1)}, u32[]{:S(2)}, u32[]{:S(2)}) collective-permute-start(bf16[320,1280]{1,0:T(8,128)(2,1)} %collective-permute-done.15.refs_5_), channel_id=1, source_target_pairs={{0,96},{32,0},{64,32},{96,64},{1,97},{33,1},{65,33},{97,65},{2,98}... | collective-permute-start | bytes 2457608 | tf_op jit(solution)/shard_map/ppermute | solution.py:226
  91.1 11.6 %collective-permute-done.14.refs_4_ = bf16[320,1280]{1,0:T(8,128)(2,1)} collective-permute-done((bf16[320,1280]{1,0:T(8,128)(2,1)}, bf16[320,1280]{1,0:T(8,128)(2,1)}, u32[]{:S(2)}, u32[]{:S(2)}) %collective-permute-start.14) | collective-permute-done | bytes 819232 | tf_op jit(solution)/shard_map/ppermute | solution.py:226
  102.7 2.9 %collective-permute-done.12.refs_3_ = bf16[320,1280]{1,0:T(8,128)(2,1)S(1)} collective-permute-done((bf16[320,1280]{1,0:T(8,128)(2,1)S(1)}, bf16[320,1280]{1,0:T(8,128)(2,1)S(1)}, u32[]{:S(2)}, u32[]{:S(2)}) %collective-permute-start.12) | collective-permute-done | bytes 819232 | tf_op jit(solution)/shard_map/ppermute | solution.py:226
  105.6 3.4 %collective-permute-start.13 = (bf16[320,1280]{1,0:T(8,128)(2,1)S(1)}, bf16[320,1280]{1,0:T(8,128)(2,1)}, u32[]{:S(2)}, u32[]{:S(2)}) collective-permute-start(bf16[320,1280]{1,0:T(8,128)(2,1)S(1)} %collective-permute-done.12.refs_3_), channel_id=1, source_target_pairs={{0,96},{32,0},{64,32},{96,64},{1,97},{33,1},{65,33},{97,65},{2,98}... | collective-permute-start | bytes 2457608 | tf_op jit(solution)/shard_map/ppermute | solution.py:226
  109.0 11.2 %collective-permute-done.16.refs_6_ = bf16[320,1280]{1,0:T(8,128)(2,1)S(1)} collective-permute-done((bf16[320,1280]{1,0:T(8,128)(2,1)}, bf16[320,1280]{1,0:T(8,128)(2,1)S(1)}, u32[]{:S(2)}, u32[]{:S(2)}) %collective-permute-start.16) | collective-permute-done | bytes 819232 | tf_op jit(solution)/shard_map/ppermute | solution.py:226
  120.2 3.1 %collective-permute-done.17.refs_7_ = bf16[320,1280]{1,0:T(8,128)(2,1)S(1)} collective-permute-done((bf16[320,1280]{1,0:T(8,128)(2,1)}, bf16[320,1280]{1,0:T(8,128)(2,1)S(1)}, u32[]{:S(2)}, u32[]{:S(2)}) %collective-permute-start.17) | collective-permute-done | bytes 819232 | tf_op jit(solution)/shard_map/ppermute | solution.py:226
  123.2 3.3 %collective-permute-start.23 = (bf16[320,1280]{1,0:T(8,128)(2,1)}, bf16[320,1280]{1,0:T(8,128)(2,1)}, u32[]{:S(2)}, u32[]{:S(2)}) collective-permute-start(bf16[320,1280]{1,0:T(8,128)(2,1)} %collective-permute-done.21.refs_5_), channel_id=1, source_target_pairs={{0,96},{32,0},{64,32},{96,64},{1,97},{33,1},{65,33},{97,65},{2,98}... | collective-permute-start | bytes 2457608 | tf_op jit(solution)/shard_map/ppermute | solution.py:226
  126.5 1.7 copy-done.2
  128.3 1.1 copy-done.8
  129.4 11.1 %expert_part.3 = (bf16[256,1280]{1,0:T(8,128)(2,1)S(1)}, bf16[256,1280]{1,0:T(8,128)(2,1)S(1)}, f32[2,1280]{1,0:T(2,128)S(1)}) custom-call(s32[4]{0:T(128)S(1)} %pad_add_fusion.where_ref.refs_0_, bf16[320,1280]{1,0:T(8,128)(2,1)} %bitcast.6.refs_1_, bf16[320,1280]{1,0:T(8,128)(2,1)} %collective-permute-done.9.refs_2_, bf16[320,1280]{1,0:T(8,128)(2,1)S(1)} %copy-done.8, ...), custom_call_target="tpu_custom_call" | custom-call | tf_op jit(solution)/shard_map/expert_part/pallas_call | solution.py:169
  140.6 0.8 copy-done.9
  141.4 0.8 copy-done.15
  142.3 2.8 %collective-permute-start.25 = (bf16[256,1280]{1,0:T(8,128)(2,1)}, bf16[256,1280]{1,0:T(8,128)(2,1)}, u32[]{:S(2)}, u32[]{:S(2)}) collective-permute-start(bf16[256,1280]{1,0:T(8,128)(2,1)} %copy-done.15), channel_id=1, source_target_pairs={{0,16},{16,0},{1,17},{17,1},{2,18},{18,2},{3,19},{19,3},{4,20},{20... | collective-permute-start | bytes 1966088 | tf_op jit(solution)/shard_map/ppermute | solution.py:226
  145.1 1.7 copy-done.3
  146.8 1.1 copy-done.5
  148.0 5.0 %expert_part.4 = f32[1,1280]{1,0:T(1,128)S(1)} custom-call(s32[4]{0:T(128)S(1)} %pad_add_fusion.where_ref.refs_0_, bf16[320,1280]{1,0:T(8,128)(2,1)S(1)} %bitcast.33, bf16[320,1280]{1,0:T(8,128)(2,1)} %collective-permute-done.20.refs_2_, bf16[320,1280]{1,0:T(8,128)(2,1)S(1)} %copy-done.5, bf16[320,1280]{1,0:T(8,128)(2,1)} %collective-permute-done.13.refs_4_, ...), custom_call_target="tpu_custom_call" | custom-call | tf_op jit(solution)/shard_map/expert_part/pallas_call | solution.py:169
  153.0 3.8 %collective-permute-done.22.refs_6_ = bf16[320,1280]{1,0:T(8,128)(2,1)} collective-permute-done((bf16[320,1280]{1,0:T(8,128)(2,1)}, bf16[320,1280]{1,0:T(8,128)(2,1)}, u32[]{:S(2)}, u32[]{:S(2)}) %collective-permute-start.22) | collective-permute-done | bytes 819232 | tf_op jit(solution)/shard_map/ppermute | solution.py:226
  156.8 1.6 collective-permute-done.23.refs_7_
  158.3 1.5 collective-permute-done.24.refs_8_
  159.8 10.4 %expert_part.5 = (bf16[256,1280]{1,0:T(8,128)(2,1)S(1)}, bf16[256,1280]{1,0:T(8,128)(2,1)}, f32[1,1280]{1,0:T(1,128)S(1)}) custom-call(s32[4]{0:T(128)S(1)} %pad_add_fusion.where_ref.refs_0_, bf16[320,1280]{1,0:T(8,128)(2,1)S(1)} %bitcast.34, bf16[320,1280]{1,0:T(8,128)(2,1)} %collective-permute-done.20.refs_2_, bf16[320,1280]{1,0:T(8,128)(2,1)S(1)} %copy-done.5, ...), custom_call_target="tpu_custom_call" | custom-call | tf_op jit(solution)/shard_map/expert_part/pallas_call | solution.py:169
  170.3 0.8 copy-done.11
  171.1 3.4 %collective-permute-start.26 = (bf16[256,1280]{1,0:T(8,128)(2,1)}, bf16[256,1280]{1,0:T(8,128)(2,1)S(1)}, u32[]{:S(2)}, u32[]{:S(2)}) collective-permute-start(bf16[256,1280]{1,0:T(8,128)(2,1)} %get-tuple-element.49), channel_id=1, source_target_pairs={{0,16},{16,0},{1,17},{17,1},{2,18},{18,2},{3,19},{19,3},{4,20},{20... | collective-permute-start | bytes 1966088 | tf_op jit(solution)/shard_map/ppermute | solution.py:226
  174.6 0.5 fusion.1
  175.3 9.2 %all_to_all.32 = f32[16,1,160]{2,1,0:T(1,128)S(1)} all-to-all(f32[16,1,160]{2,1,0:T(1,128)S(1)} %all_to_all.27), channel_id=1, replica_groups=mesh['x_lo'=2,'y'=4,'core'=2,'x_hi'=2,'z'=8] {'x_lo','y','core'}, dimensions={0} | all-to-all | bytes 20480 | tf_op jit(solution)/shard_map/all_to_all | solution.py:313
  184.6 0.7 all_to_all.24
  185.3 6.7 %all-to-all-start.3 = ((f32[16,1,10]{2,1,0:T(1,128)}), f32[16,1,10]{2,1,0:T(1,128)S(1)}, u32[]{:S(2)}, u32[]{:S(2)}) async-start(f32[16,1,10]{2,1,0:T(1,128)} %bitcast.14), calls=%async_computation.3 | async-start | bytes 16384 | tf_op jit(solution)/shard_map/all_to_all | solution.py:315
  192.0 1.1 copy-done.10
  193.1 1.1 copy-done.12
  194.2 3.3 %join.1 = bf16[256,5120]{1,0:T(8,128)(2,1)} custom-call(s32[4]{0:T(128)S(1)} %pad_add_fusion.where_ref.refs_0_, bf16[256,1280]{1,0:T(8,128)(2,1)S(1)} %copy-done.10, bf16[256,1280]{1,0:T(8,128)(2,1)S(1)} %copy-done.12, bf16[256,1280]{1,0:T(8,128)(2,1)} %collective-permute-done.25.refs_3_, bf16[256,1280]{1,0:T(8,128)(2,1)S(1)} %collective-permute-done.26.refs_4_), custom_call_target="tpu_custom_call" | custom-call | tf_op jit(solution)/shard_map/join/pallas_call | solution.py:208
  197.5 3.3 %all-to-all-done.3 = f32[16,1,10]{2,1,0:T(1,128)S(1)} async-done(((f32[16,1,10]{2,1,0:T(1,128)}), f32[16,1,10]{2,1,0:T(1,128)S(1)}, u32[]{:S(2)}, u32[]{:S(2)}) %all-to-all-start.3) | async-done | bytes 672 | tf_op jit(solution)/shard_map/all_to_all | solution.py:315
  201.0 0.5 fusion.6
  (63 shorter events, 1.0 us)
Async XLA Ops:
  0.6 7.7 %copy-start.18 = (s32[128,1]{0,1:T(1,128)S(1)}, s32[128,1]{0,1:T(1,128)}, u32[]{:S(2)}) copy-start(s32[128,1]{0,1:T(1,128)} %param.7) | copy-start | bytes 1540
  2.0 9.5 %collective-permute-start.3 = (bf16[128,1280]{1,0:T(8,128)(2,1)S(1)}, bf16[128,1280]{1,0:T(8,128)(2,1)S(1)}, u32[]{:S(2)}, u32[]{:S(2)}) collective-permute-start(bf16[128,1280]{1,0:T(8,128)(2,1)S(1)} %get-tuple-element.52), channel_id=1, source_target_pairs={{0,16},{16,0},{1,17},{17,1},{2,18},{18,2},{3,19},{19,3},{4,20},{20... | collective-permute-start | bytes 983048 | tf_op jit(solution)/shard_map/ppermute | solution.py:226
  5.3 10.5 %collective-permute-start.4 = (bf16[128,1280]{1,0:T(8,128)(2,1)S(1)}, bf16[128,1280]{1,0:T(8,128)(2,1)S(1)}, u32[]{:S(2)}, u32[]{:S(2)}) collective-permute-start(bf16[128,1280]{1,0:T(8,128)(2,1)S(1)} %get-tuple-element.29.t0), channel_id=1, source_target_pairs={{0,136},{8,128},{16,152},{24,144},{128,8},{136,0},{144,24},{152,16... | collective-permute-start | bytes 983048 | tf_op jit(solution)/shard_map/ppermute | solution.py:236
  6.1 17.0 %collective-permute-start.5 = (bf16[128,1280]{1,0:T(8,128)(2,1)S(1)}, bf16[128,1280]{1,0:T(8,128)(2,1)S(1)}, u32[]{:S(2)}, u32[]{:S(2)}) collective-permute-start(bf16[128,1280]{1,0:T(8,128)(2,1)S(1)} %get-tuple-element.52), channel_id=1, source_target_pairs={{0,152},{8,144},{16,136},{24,128},{128,24},{136,16},{144,8},{152,0... | collective-permute-start | bytes 983048 | tf_op jit(solution)/shard_map/ppermute | solution.py:236
  10.6 12.5 %collective-permute-start = (f32[8,128]{1,0:T(8,128)}, f32[8,128]{1,0:T(8,128)S(1)}, u32[]{:S(2)}, u32[]{:S(2)}) collective-permute-start(f32[8,128]{1,0:T(8,128)} %route.1.m0), channel_id=1, source_target_pairs={{0,16},{16,0},{1,17},{17,1},{2,18},{18,2},{3,19},{19,3},{4,20},{20... | collective-permute-start | bytes 12296 | tf_op jit(solution)/shard_map/ppermute | solution.py:226
  10.7 12.4 %collective-permute-start.1 = (f32[8,128]{1,0:T(8,128)}, f32[8,128]{1,0:T(8,128)S(1)}, u32[]{:S(2)}, u32[]{:S(2)}) collective-permute-start(f32[8,128]{1,0:T(8,128)} %route.1.m0), channel_id=1, source_target_pairs={{0,136},{8,128},{16,152},{24,144},{128,8},{136,0},{144,24},{152,16... | collective-permute-start | bytes 12296 | tf_op jit(solution)/shard_map/ppermute | solution.py:236
  11.5 12.0 %collective-permute-start.2 = (f32[8,128]{1,0:T(8,128)}, f32[8,128]{1,0:T(8,128)S(1)}, u32[]{:S(2)}, u32[]{:S(2)}) collective-permute-start(f32[8,128]{1,0:T(8,128)} %route.1.m0), channel_id=1, source_target_pairs={{0,152},{8,144},{16,136},{24,128},{128,24},{136,16},{144,8},{152,0... | collective-permute-start | bytes 12296 | tf_op jit(solution)/shard_map/ppermute | solution.py:236
  23.5 0.7 copy-start.13
  26.6 24.8 %copy-start.14 = (f32[8,128]{1,0:T(8,128)S(1)}, f32[8,128]{1,0:T(8,128)}, u32[]{:S(2)}) copy-start(f32[8,128]{1,0:T(8,128)} %route.1.m0) | copy-start | bytes 12292
  26.7 30.8 %all-to-all-start = ((bf16[8,40,1280]{2,1,0:T(8,128)(2,1)}), bf16[8,40,1280]{2,1,0:T(8,128)(2,1)}, u32[]{:S(2)}, u32[]{:S(2)}) async-start(bf16[8,40,1280]{2,1,0:T(8,128)(2,1)} %bitcast.5), calls=%async_computation | async-start | bytes 1638400 | tf_op jit(solution)/shard_map/all_to_all | solution.py:271
  33.1 3.8 %collective-permute-start.6 = (bf16[128,1280]{1,0:T(8,128)(2,1)S(1)}, bf16[128,1280]{1,0:T(8,128)(2,1)S(1)}, u32[]{:S(2)}, u32[]{:S(2)}) collective-permute-start(bf16[128,1280]{1,0:T(8,128)(2,1)S(1)} %get-tuple-element.28), channel_id=1, source_target_pairs={{0,16},{16,0},{1,17},{17,1},{2,18},{18,2},{3,19},{19,3},{4,20},{20... | collective-permute-start | bytes 983048 | tf_op jit(solution)/shard_map/ppermute | solution.py:226
  33.8 10.6 %collective-permute-start.7 = (bf16[128,1280]{1,0:T(8,128)(2,1)S(1)}, bf16[128,1280]{1,0:T(8,128)(2,1)S(1)}, u32[]{:S(2)}, u32[]{:S(2)}) collective-permute-start(bf16[128,1280]{1,0:T(8,128)(2,1)S(1)} %get-tuple-element.27.t0), channel_id=1, source_target_pairs={{0,136},{8,128},{16,152},{24,144},{128,8},{136,0},{144,24},{152,16... | collective-permute-start | bytes 983048 | tf_op jit(solution)/shard_map/ppermute | solution.py:236
  36.3 15.2 %collective-permute-start.8 = (bf16[128,1280]{1,0:T(8,128)(2,1)S(1)}, bf16[128,1280]{1,0:T(8,128)(2,1)S(1)}, u32[]{:S(2)}, u32[]{:S(2)}) collective-permute-start(bf16[128,1280]{1,0:T(8,128)(2,1)S(1)} %get-tuple-element.28), channel_id=1, source_target_pairs={{0,152},{8,144},{16,136},{24,128},{128,24},{136,16},{144,8},{152,0... | collective-permute-start | bytes 983048 | tf_op jit(solution)/shard_map/ppermute | solution.py:236
  36.7 29.4 %collective-permute-start.10 = (bf16[2560,256]{1,0:T(8,128)(2,1)}, bf16[2560,256]{1,0:T(8,128)(2,1)}, u32[]{:S(2)}, u32[]{:S(2)}) collective-permute-start(bf16[2560,256]{1,0:T(8,128)(2,1)} %bitcast.9.own_ref), channel_id=1, source_target_pairs={{0,16},{16,0},{1,17},{17,1},{2,18},{18,2},{3,19},{19,3},{4,20},{20... | collective-permute-start | bytes 3932168 | tf_op jit(solution)/shard_map/ppermute | solution.py:226
  51.5 12.7 %copy-start = (bf16[1,256,5120]{2,1,0:T(8,128)(2,1)S(1)}, bf16[1,256,5120]{2,1,0:T(8,128)(2,1)}, u32[]{:S(2)}) copy-start(bf16[1,256,5120]{2,1,0:T(8,128)(2,1)} %param.10) | copy-start | bytes 7864324
  53.1 0.9 copy-start.6
  57.5 28.2 %all-to-all-start.1 = ((bf16[8,40,1280]{2,1,0:T(8,128)(2,1)}), bf16[8,40,1280]{2,1,0:T(8,128)(2,1)S(1)}, u32[]{:S(2)}, u32[]{:S(2)}) async-start(bf16[8,40,1280]{2,1,0:T(8,128)(2,1)} %bitcast.35), calls=%async_computation.1 | async-start | bytes 1638400 | tf_op jit(solution)/shard_map/all_to_all | solution.py:271
  61.3 21.2 %collective-permute-start.9 = (bf16[320,1280]{1,0:T(8,128)(2,1)}, bf16[320,1280]{1,0:T(8,128)(2,1)}, u32[]{:S(2)}, u32[]{:S(2)}) collective-permute-start(bf16[320,1280]{1,0:T(8,128)(2,1)} %bitcast.6.refs_1_), channel_id=1, source_target_pairs={{0,32},{32,64},{64,96},{96,0},{1,33},{33,65},{65,97},{97,1},{2,34}... | collective-permute-start | bytes 2457608 | tf_op jit(solution)/shard_map/ppermute | solution.py:226
  62.6 19.9 %collective-permute-start.11 = (bf16[320,1280]{1,0:T(8,128)(2,1)}, bf16[320,1280]{1,0:T(8,128)(2,1)S(1)}, u32[]{:S(2)}, u32[]{:S(2)}) collective-permute-start(bf16[320,1280]{1,0:T(8,128)(2,1)} %bitcast.6.refs_1_), channel_id=1, source_target_pairs={{0,96},{32,0},{64,32},{96,64},{1,97},{33,1},{65,33},{97,65},{2,98}... | collective-permute-start | bytes 2457608 | tf_op jit(solution)/shard_map/ppermute | solution.py:226
  64.1 2.0 copy-start.16
  65.4 23.1 %collective-permute-start.19 = (bf16[256,2560]{1,0:T(8,128)(2,1)}, bf16[256,2560]{1,0:T(8,128)(2,1)}, u32[]{:S(2)}, u32[]{:S(2)}) collective-permute-start(bf16[256,2560]{1,0:T(8,128)(2,1)} %slice_select_fusion), channel_id=1, source_target_pairs={{0,16},{16,0},{1,17},{17,1},{2,18},{18,2},{3,19},{19,3},{4,20},{20... | collective-permute-start | bytes 3932168 | tf_op jit(solution)/shard_map/ppermute | solution.py:226
  66.1 22.3 %collective-permute-start.15 = (bf16[320,1280]{1,0:T(8,128)(2,1)}, bf16[320,1280]{1,0:T(8,128)(2,1)}, u32[]{:S(2)}, u32[]{:S(2)}) collective-permute-start(bf16[320,1280]{1,0:T(8,128)(2,1)} %bitcast.6.refs_1_), channel_id=1, source_target_pairs={{0,128},{128,0},{1,129},{129,1},{2,130},{130,2},{3,131},{131,3},{4... | collective-permute-start | bytes 2457608 | tf_op jit(solution)/shard_map/ppermute | solution.py:226
  70.6 1.5 copy-start.1
  82.5 20.2 %collective-permute-start.14 = (bf16[320,1280]{1,0:T(8,128)(2,1)}, bf16[320,1280]{1,0:T(8,128)(2,1)}, u32[]{:S(2)}, u32[]{:S(2)}) collective-permute-start(bf16[320,1280]{1,0:T(8,128)(2,1)} %collective-permute-done.9.refs_2_), channel_id=1, source_target_pairs={{0,32},{32,64},{64,96},{96,0},{1,33},{33,65},{65,97},{97,1},{2,34}... | collective-permute-start | bytes 2457608 | tf_op jit(solution)/shard_map/ppermute | solution.py:226
  82.5 0.9 copy-start.7
  85.7 19.9 %collective-permute-start.12 = (bf16[320,1280]{1,0:T(8,128)(2,1)S(1)}, bf16[320,1280]{1,0:T(8,128)(2,1)S(1)}, u32[]{:S(2)}, u32[]{:S(2)}) collective-permute-start(bf16[320,1280]{1,0:T(8,128)(2,1)S(1)} %bitcast.30), channel_id=1, source_target_pairs={{0,96},{32,0},{64,32},{96,64},{1,97},{33,1},{65,33},{97,65},{2,98}... | collective-permute-start | bytes 2457608 | tf_op jit(solution)/shard_map/ppermute | solution.py:226
  88.4 31.7 %collective-permute-start.16 = (bf16[320,1280]{1,0:T(8,128)(2,1)}, bf16[320,1280]{1,0:T(8,128)(2,1)S(1)}, u32[]{:S(2)}, u32[]{:S(2)}) collective-permute-start(bf16[320,1280]{1,0:T(8,128)(2,1)} %collective-permute-done.15.refs_5_), channel_id=1, source_target_pairs={{0,32},{32,64},{64,96},{96,0},{1,33},{33,65},{65,97},{97,1},{2,34}... | collective-permute-start | bytes 2457608 | tf_op jit(solution)/shard_map/ppermute | solution.py:226
  88.4 31.7 %collective-permute-start.21 = (bf16[320,1280]{1,0:T(8,128)(2,1)S(1)}, bf16[320,1280]{1,0:T(8,128)(2,1)}, u32[]{:S(2)}, u32[]{:S(2)}) collective-permute-start(bf16[320,1280]{1,0:T(8,128)(2,1)S(1)} %bitcast.31), channel_id=1, source_target_pairs={{0,128},{128,0},{1,129},{129,1},{2,130},{130,2},{3,131},{131,3},{4... | collective-permute-start | bytes 2457608 | tf_op jit(solution)/shard_map/ppermute | solution.py:226
  88.4 34.8 %collective-permute-start.17 = (bf16[320,1280]{1,0:T(8,128)(2,1)}, bf16[320,1280]{1,0:T(8,128)(2,1)S(1)}, u32[]{:S(2)}, u32[]{:S(2)}) collective-permute-start(bf16[320,1280]{1,0:T(8,128)(2,1)} %collective-permute-done.15.refs_5_), channel_id=1, source_target_pairs={{0,96},{32,0},{64,32},{96,64},{1,97},{33,1},{65,33},{97,65},{2,98}... | collective-permute-start | bytes 2457608 | tf_op jit(solution)/shard_map/ppermute | solution.py:226
  102.7 23.8 %collective-permute-start.18 = (bf16[320,1280]{1,0:T(8,128)(2,1)}, bf16[320,1280]{1,0:T(8,128)(2,1)S(1)}, u32[]{:S(2)}, u32[]{:S(2)}) collective-permute-start(bf16[320,1280]{1,0:T(8,128)(2,1)} %collective-permute-done.14.refs_4_), channel_id=1, source_target_pairs={{0,128},{128,0},{1,129},{129,1},{2,130},{130,2},{3,131},{131,3},{4... | collective-permute-start | bytes 2457608 | tf_op jit(solution)/shard_map/ppermute | solution.py:226
  105.6 35.0 %copy-start.4 = (bf16[320,1280]{1,0:T(8,128)(2,1)}, bf16[320,1280]{1,0:T(8,128)(2,1)S(1)}, u32[]{:S(2)}) copy-start(bf16[320,1280]{1,0:T(8,128)(2,1)S(1)} %collective-permute-done.12.refs_3_) | copy-start | bytes 2457604
  105.6 36.7 %collective-permute-start.13 = (bf16[320,1280]{1,0:T(8,128)(2,1)S(1)}, bf16[320,1280]{1,0:T(8,128)(2,1)}, u32[]{:S(2)}, u32[]{:S(2)}) collective-permute-start(bf16[320,1280]{1,0:T(8,128)(2,1)S(1)} %collective-permute-done.12.refs_3_), channel_id=1, source_target_pairs={{0,96},{32,0},{64,32},{96,64},{1,97},{33,1},{65,33},{97,65},{2,98}... | collective-permute-start | bytes 2457608 | tf_op jit(solution)/shard_map/ppermute | solution.py:226
  120.1 24.9 %collective-permute-start.20 = (bf16[320,1280]{1,0:T(8,128)(2,1)S(1)}, bf16[320,1280]{1,0:T(8,128)(2,1)}, u32[]{:S(2)}, u32[]{:S(2)}) collective-permute-start(bf16[320,1280]{1,0:T(8,128)(2,1)S(1)} %bitcast.32), channel_id=1, source_target_pairs={{0,32},{32,64},{64,96},{96,0},{1,33},{33,65},{65,97},{97,1},{2,34}... | collective-permute-start | bytes 2457608 | tf_op jit(solution)/shard_map/ppermute | solution.py:226
  120.1 36.6 %collective-permute-start.22 = (bf16[320,1280]{1,0:T(8,128)(2,1)}, bf16[320,1280]{1,0:T(8,128)(2,1)}, u32[]{:S(2)}, u32[]{:S(2)}) collective-permute-start(bf16[320,1280]{1,0:T(8,128)(2,1)} %collective-permute-done.21.refs_5_), channel_id=1, source_target_pairs={{0,32},{32,64},{64,96},{96,0},{1,33},{33,65},{65,97},{97,1},{2,34}... | collective-permute-start | bytes 2457608 | tf_op jit(solution)/shard_map/ppermute | solution.py:226
  123.2 35.1 %collective-permute-start.23 = (bf16[320,1280]{1,0:T(8,128)(2,1)}, bf16[320,1280]{1,0:T(8,128)(2,1)}, u32[]{:S(2)}, u32[]{:S(2)}) collective-permute-start(bf16[320,1280]{1,0:T(8,128)(2,1)} %collective-permute-done.21.refs_5_), channel_id=1, source_target_pairs={{0,96},{32,0},{64,32},{96,64},{1,97},{33,1},{65,33},{97,65},{2,98}... | collective-permute-start | bytes 2457608 | tf_op jit(solution)/shard_map/ppermute | solution.py:226
  126.5 1.7 copy-start.2
  128.3 1.1 copy-start.8
  140.6 0.8 copy-start.9
  141.4 0.8 copy-start.15
  142.3 17.6 %collective-permute-start.24 = (bf16[320,1280]{1,0:T(8,128)(2,1)}, bf16[320,1280]{1,0:T(8,128)(2,1)}, u32[]{:S(2)}, u32[]{:S(2)}) collective-permute-start(bf16[320,1280]{1,0:T(8,128)(2,1)} %collective-permute-done.13.refs_4_), channel_id=1, source_target_pairs={{0,128},{128,0},{1,129},{129,1},{2,130},{130,2},{3,131},{131,3},{4... | collective-permute-start | bytes 2457608 | tf_op jit(solution)/shard_map/ppermute | solution.py:226
  142.3 49.7 %collective-permute-start.25 = (bf16[256,1280]{1,0:T(8,128)(2,1)}, bf16[256,1280]{1,0:T(8,128)(2,1)}, u32[]{:S(2)}, u32[]{:S(2)}) collective-permute-start(bf16[256,1280]{1,0:T(8,128)(2,1)} %copy-done.15), channel_id=1, source_target_pairs={{0,16},{16,0},{1,17},{17,1},{2,18},{18,2},{3,19},{19,3},{4,20},{20... | collective-permute-start | bytes 1966088 | tf_op jit(solution)/shard_map/ppermute | solution.py:226
  145.1 1.7 copy-start.3
  146.8 1.1 copy-start.5
  153.0 21.6 %copy-start.19 = (s32[2,2,80]{2,1,0:T(2,128)S(1)}, s32[2,2,80]{2,1,0:T(2,128)}, u32[]{:S(2)}) copy-start(s32[2,2,80]{2,1,0:T(2,128)} %constant.37) | copy-start | bytes 3844
  170.2 0.8 copy-start.11
  171.1 20.9 %collective-permute-start.26 = (bf16[256,1280]{1,0:T(8,128)(2,1)}, bf16[256,1280]{1,0:T(8,128)(2,1)S(1)}, u32[]{:S(2)}, u32[]{:S(2)}) collective-permute-start(bf16[256,1280]{1,0:T(8,128)(2,1)} %get-tuple-element.49), channel_id=1, source_target_pairs={{0,16},{16,0},{1,17},{17,1},{2,18},{18,2},{3,19},{19,3},{4,20},{20... | collective-permute-start | bytes 1966088 | tf_op jit(solution)/shard_map/ppermute | solution.py:226
  185.3 15.5 %all-to-all-start.3 = ((f32[16,1,10]{2,1,0:T(1,128)}), f32[16,1,10]{2,1,0:T(1,128)S(1)}, u32[]{:S(2)}, u32[]{:S(2)}) async-start(f32[16,1,10]{2,1,0:T(1,128)} %bitcast.14), calls=%async_computation.3 | async-start | bytes 16384 | tf_op jit(solution)/shard_map/all_to_all | solution.py:315
  192.0 1.1 copy-start.10
  193.1 1.1 copy-start.12
  194.2 6.8 %copy-start.17 = (f32[128]{0:T(128)S(1)}, f32[128]{0:T(128)}, u32[]{:S(2)}) copy-start(f32[128]{0:T(128)} %param.8) | copy-start | bytes 1540

commit v2 on v1

--- a/solution.py
+++ b/solution.py
@@ -50,10 +50,7 @@
     )(ids, logit.reshape(1, TOK))
 
 
-def place_kernel(where_ref, m0, m1, m2, m3, t0, t1, t2, t3, out_ref, toks, sems):
-    copies = [pltpu.make_async_copy(t, toks.at[i], sems.at[i]) for i, t in enumerate((t0, t1, t2, t3))]
-    for copy in copies:
-        copy.start()
+def place_kernel(where_ref, m0, m1, m2, m3, t0, t1, t2, t3, out_ref):
     core, x_hi = where_ref[0], where_ref[1]
     slot = lax.broadcasted_iota(jnp.int32, (BLOCK, TOK), 0).astype(F32)
     first = (8 * x_hi).astype(F32)
@@ -65,12 +62,10 @@
         z = meta[0:1, :] - first
         pos = jnp.where((z >= 0.0) & (z < 8.0), z * 40.0 + meta[1:2, :] + base, -1.0)
         hots.append(jnp.where(slot == pos, meta[2:3, :], 0.0).astype(BF))
-    for copy in copies:
-        copy.wait()
     total = None
-    for i in range(2):
+    for i, (low, high) in enumerate(((t0, t1), (t2, t3))):
         hot = jnp.concatenate(hots[2 * i : 2 * i + 2], axis=1)
-        pair = toks[2 * i : 2 * i + 2].reshape(2 * TOK, toks.shape[2])
+        pair = jnp.concatenate([low[...], high[...]], axis=0)
         part = jnp.dot(hot, pair, preferred_element_type=F32)
         total = part if total is None else total + part
     out_ref[...] = total.astype(BF)
@@ -81,9 +76,8 @@
     return pl.pallas_call(
         place_kernel,
         out_shape=jax.ShapeDtypeStruct((BLOCK, width), BF),
-        in_specs=[SMEM] + [VMEM] * 4 + [ANY] * 4,
+        in_specs=[SMEM] + [VMEM] * 8,
         out_specs=VMEM,
-        scratch_shapes=[pltpu.VMEM((4, TOK, width), BF), pltpu.SemaphoreType.DMA((4,))],
         compiler_params=pltpu.CompilerParams(vmem_limit_bytes=16 * MIB),
         cost_estimate=pl.CostEstimate(
             flops=2 * 4 * BLOCK * TOK * width, bytes_accessed=2 * width * (4 * TOK + BLOCK), transcendentals=0

time: 202 us -> 202 us (level)
  transfers between devices with their start and end apart: 30 -> 30, of which waited for: 16 -> 16; matrix products, arithmetic and copies ran while one was open for 1% -> 1% of each run, Pallas kernels for 19% -> 18%
where the time goes in v2:
time: 202 us; the launch traced here: 201 us
  waiting for transfers between devices  79 us (39%)
  starting transfers between devices  53.1 us (26%)
  Pallas kernels  38.9 us (19%)
  local copies, waits for them, and re-layouts  16.1 us (8%)
  blocking collectives  9.2 us (5%)
  other arithmetic  3.46 us (2%)
    ppermute x21, waiting for transfers between devices, send(): lax.ppermute(array, axis, [(i, (i + shift) % size) for i in range(size)])  45.4 us
    ppermute x21, starting transfers between devices, send(): lax.ppermute(array, axis, [(i, (i + shift) % size) for i in range(size)])  26.6 us
    pallas_call x3, Pallas kernels, expert_part(): pl.pallas_call(lambda *refs: expert_kernel(off, width, places, sides, gra...  26.5 us
    ppermute x6, waiting for transfers between devices, send(): return lax.ppermute(array, axes, [(i, i ^ flip) for i in range(8)])  24 us
    unnamed x41, local copies, waits for them, and re-layouts  15.2 us
    all_to_all x2, starting transfers between devices, spread(): lax.all_to_all(sent.reshape(8, 40, width), 'z', split_axis=0, concat_axis...  10.1 us
    all_to_all x1, blocking collectives, body(): lax.all_to_all(parts, ('x_lo', 'y', 'core'), split_axis=0, concat_axis=0,...  9.2 us
    ppermute x6, starting transfers between devices, send(): return lax.ppermute(array, axes, [(i, i ^ flip) for i in range(8)])  9.08 us
  transfers between devices with their start and end apart: 30, of which 16 were waited for; matrix products, arithmetic and copies ran while one was open for 1% of the time, Pallas kernels for 18%

profile of v2, /device:TPU:1, one launch (start us, length us, event | category | flops | bytes accessed | tf_op | source)
XLA Modules:
  0.0 201.2 jit_solution(13701549879017603921)
XLA Ops:
  0.6 1.4 broadcast_select_fusion
  2.0 3.3 %collective-permute-start.3 = (bf16[128,1280]{1,0:T(8,128)(2,1)S(1)}, bf16[128,1280]{1,0:T(8,128)(2,1)S(1)}, u32[]{:S(2)}, u32[]{:S(2)}) collective-permute-start(bf16[128,1280]{1,0:T(8,128)(2,1)S(1)} %get-tuple-element.52), channel_id=1, source_target_pairs={{0,16},{16,0},{1,17},{17,1},{2,18},{18,2},{3,19},{19,3},{4,20},{20... | collective-permute-start | bytes 983048 | tf_op jit(solution)/shard_map/ppermute | solution.py:220
  5.3 0.8 collective-permute-start.4
  6.1 2.2 %collective-permute-start.5 = (bf16[128,1280]{1,0:T(8,128)(2,1)S(1)}, bf16[128,1280]{1,0:T(8,128)(2,1)S(1)}, u32[]{:S(2)}, u32[]{:S(2)}) collective-permute-start(bf16[128,1280]{1,0:T(8,128)(2,1)S(1)} %get-tuple-element.52), channel_id=1, source_target_pairs={{0,152},{8,144},{16,136},{24,128},{128,24},{136,16},{144,8},{152,0... | collective-permute-start | bytes 983048 | tf_op jit(solution)/shard_map/ppermute | solution.py:230
  8.3 0.7 copy.15.ids_ref
  9.0 1.5 route.1.m0
  10.7 0.7 collective-permute-start.1
  11.5 2.5 %collective-permute-start.2 = (f32[8,128]{1,0:T(8,128)}, f32[8,128]{1,0:T(8,128)S(1)}, u32[]{:S(2)}, u32[]{:S(2)}) collective-permute-start(f32[8,128]{1,0:T(8,128)} %route.1.m0), channel_id=1, source_target_pairs={{0,152},{8,144},{16,136},{24,128},{128,24},{136,16},{144,8},{152,0... | collective-permute-start | bytes 12296 | tf_op jit(solution)/shard_map/ppermute | solution.py:230
  14.0 1.8 collective-permute-done.4.t2
  15.8 7.3 %collective-permute-done.5.t3 = bf16[128,1280]{1,0:T(8,128)(2,1)S(1)} collective-permute-done((bf16[128,1280]{1,0:T(8,128)(2,1)S(1)}, bf16[128,1280]{1,0:T(8,128)(2,1)S(1)}, u32[]{:S(2)}, u32[]{:S(2)}) %collective-permute-start.5) | collective-permute-done | bytes 327712 | tf_op jit(solution)/shard_map/ppermute | solution.py:230
  23.1 0.3 collective-permute-done.2.m3
  23.5 0.7 copy-done.13
  24.1 2.0 %place.3 = bf16[320,1280]{1,0:T(8,128)(2,1)} custom-call(s32[4]{0:T(128)S(1)} %pad_add_fusion.where_ref.refs_0_, f32[8,128]{1,0:T(8,128)S(1)} %copy-done.13, f32[8,128]{1,0:T(8,128)S(1)} %collective-permute-done.m1, f32[8,128]{1,0:T(8,128)S(1)} %collective-permute-done.1.m2, f32[8,128]{1,0:T(8,128)S(1)} %collective-permute-done.2.m3, ...), custom_call_target="tpu_custom_call" | custom-call | flops 419430400 | bytes 2129920 | tf_op jit(solution)/shard_map/place/pallas_call | solution.py:76
  26.2 6.6 %all-to-all-start = ((bf16[8,40,1280]{2,1,0:T(8,128)(2,1)}), bf16[8,40,1280]{2,1,0:T(8,128)(2,1)}, u32[]{:S(2)}, u32[]{:S(2)}) async-start(bf16[8,40,1280]{2,1,0:T(8,128)(2,1)} %bitcast.5), calls=%async_computation | async-start | bytes 1638400 | tf_op jit(solution)/shard_map/all_to_all | solution.py:265
  32.8 0.7 collective-permute-start.6
  33.4 2.5 %collective-permute-start.7 = (bf16[128,1280]{1,0:T(8,128)(2,1)S(1)}, bf16[128,1280]{1,0:T(8,128)(2,1)S(1)}, u32[]{:S(2)}, u32[]{:S(2)}) collective-permute-start(bf16[128,1280]{1,0:T(8,128)(2,1)S(1)} %get-tuple-element.27.t0), channel_id=1, source_target_pairs={{0,136},{8,128},{16,152},{24,144},{128,8},{136,0},{144,24},{152,16... | collective-permute-start | bytes 983048 | tf_op jit(solution)/shard_map/ppermute | solution.py:230
  35.9 0.4 collective-permute-start.8
  36.5 7.5 %collective-permute-done.7.t2 = bf16[128,1280]{1,0:T(8,128)(2,1)S(1)} collective-permute-done((bf16[128,1280]{1,0:T(8,128)(2,1)S(1)}, bf16[128,1280]{1,0:T(8,128)(2,1)S(1)}, u32[]{:S(2)}, u32[]{:S(2)}) %collective-permute-start.7) | collective-permute-done | bytes 327712 | tf_op jit(solution)/shard_map/ppermute | solution.py:230
  44.0 7.1 %collective-permute-done.8.t3 = bf16[128,1280]{1,0:T(8,128)(2,1)S(1)} collective-permute-done((bf16[128,1280]{1,0:T(8,128)(2,1)S(1)}, bf16[128,1280]{1,0:T(8,128)(2,1)S(1)}, u32[]{:S(2)}, u32[]{:S(2)}) %collective-permute-start.8) | collective-permute-done | bytes 327712 | tf_op jit(solution)/shard_map/ppermute | solution.py:230
  51.1 1.1 place.2
  52.3 0.9 copy-done.6
  53.2 4.0 %all-to-all-done = bf16[8,40,1280]{2,1,0:T(8,128)(2,1)} async-done(((bf16[8,40,1280]{2,1,0:T(8,128)(2,1)}), bf16[8,40,1280]{2,1,0:T(8,128)(2,1)}, u32[]{:S(2)}, u32[]{:S(2)}) %all-to-all-start) | async-done | bytes 819232 | tf_op jit(solution)/shard_map/all_to_all | solution.py:265
  57.1 3.5 %all-to-all-start.1 = ((bf16[8,40,1280]{2,1,0:T(8,128)(2,1)}), bf16[8,40,1280]{2,1,0:T(8,128)(2,1)S(1)}, u32[]{:S(2)}, u32[]{:S(2)}) async-start(bf16[8,40,1280]{2,1,0:T(8,128)(2,1)} %bitcast.35), calls=%async_computation.1 | async-start | bytes 1638400 | tf_op jit(solution)/shard_map/all_to_all | solution.py:265
  60.7 1.4 collective-permute-start.9
  62.1 1.5 collective-permute-start.11
  63.6 1.2 slice_select_fusion
  64.8 0.9 collective-permute-start.19
  65.7 4.4 %turn.1.refs_9_.refs_5_ = bf16[512,2560]{1,0:T(8,128)(2,1)S(1)} custom-call(s32[4]{0:T(128)S(1)} %pad_add_fusion.where_ref.refs_0_, s32[640,1]{1,0:T(8,128)S(1)} %copy-done.16, bf16[2560,256]{1,0:T(8,128)(2,1)} %bitcast.9.own_ref, bf16[2560,256]{1,0:T(8,128)(2,1)} %collective-permute-done.10.par_ref), custom_call_target="tpu_custom_call" | custom-call | flops 1677721600 | bytes 5242880 | tf_op jit(solution)/shard_map/turn/pallas_call | solution.py:110
  70.2 1.5 copy-done.1
  71.7 10.1 %collective-permute-done.9.refs_2_ = bf16[320,1280]{1,0:T(8,128)(2,1)} collective-permute-done((bf16[320,1280]{1,0:T(8,128)(2,1)}, bf16[320,1280]{1,0:T(8,128)(2,1)}, u32[]{:S(2)}, u32[]{:S(2)}) %collective-permute-start.9) | collective-permute-done | bytes 819232 | tf_op jit(solution)/shard_map/ppermute | solution.py:220
  81.8 0.9 copy-done.7
  82.7 2.3 %all-to-all-done.1 = bf16[8,40,1280]{2,1,0:T(8,128)(2,1)S(1)} async-done(((bf16[8,40,1280]{2,1,0:T(8,128)(2,1)}), bf16[8,40,1280]{2,1,0:T(8,128)(2,1)S(1)}, u32[]{:S(2)}, u32[]{:S(2)}) %all-to-all-start.1) | async-done | bytes 819232 | tf_op jit(solution)/shard_map/all_to_all | solution.py:265
  84.9 2.7 %collective-permute-start.12 = (bf16[320,1280]{1,0:T(8,128)(2,1)S(1)}, bf16[320,1280]{1,0:T(8,128)(2,1)S(1)}, u32[]{:S(2)}, u32[]{:S(2)}) collective-permute-start(bf16[320,1280]{1,0:T(8,128)(2,1)S(1)} %bitcast.30), channel_id=1, source_target_pairs={{0,96},{32,0},{64,32},{96,64},{1,97},{33,1},{65,33},{97,65},{2,98}... | collective-permute-start | bytes 2457608 | tf_op jit(solution)/shard_map/ppermute | solution.py:220
  87.7 2.7 %collective-permute-start.17 = (bf16[320,1280]{1,0:T(8,128)(2,1)}, bf16[320,1280]{1,0:T(8,128)(2,1)S(1)}, u32[]{:S(2)}, u32[]{:S(2)}) collective-permute-start(bf16[320,1280]{1,0:T(8,128)(2,1)} %collective-permute-done.15.refs_5_), channel_id=1, source_target_pairs={{0,96},{32,0},{64,32},{96,64},{1,97},{33,1},{65,33},{97,65},{2,98}... | collective-permute-start | bytes 2457608 | tf_op jit(solution)/shard_map/ppermute | solution.py:220
  90.4 11.4 %collective-permute-done.14.refs_4_ = bf16[320,1280]{1,0:T(8,128)(2,1)} collective-permute-done((bf16[320,1280]{1,0:T(8,128)(2,1)}, bf16[320,1280]{1,0:T(8,128)(2,1)}, u32[]{:S(2)}, u32[]{:S(2)}) %collective-permute-start.14) | collective-permute-done | bytes 819232 | tf_op jit(solution)/shard_map/ppermute | solution.py:220
  101.7 3.0 %collective-permute-done.12.refs_3_ = bf16[320,1280]{1,0:T(8,128)(2,1)S(1)} collective-permute-done((bf16[320,1280]{1,0:T(8,128)(2,1)S(1)}, bf16[320,1280]{1,0:T(8,128)(2,1)S(1)}, u32[]{:S(2)}, u32[]{:S(2)}) %collective-permute-start.12) | collective-permute-done | bytes 819232 | tf_op jit(solution)/shard_map/ppermute | solution.py:220
  104.8 3.4 %collective-permute-start.13 = (bf16[320,1280]{1,0:T(8,128)(2,1)S(1)}, bf16[320,1280]{1,0:T(8,128)(2,1)}, u32[]{:S(2)}, u32[]{:S(2)}) collective-permute-start(bf16[320,1280]{1,0:T(8,128)(2,1)S(1)} %collective-permute-done.12.refs_3_), channel_id=1, source_target_pairs={{0,96},{32,0},{64,32},{96,64},{1,97},{33,1},{65,33},{97,65},{2,98}... | collective-permute-start | bytes 2457608 | tf_op jit(solution)/shard_map/ppermute | solution.py:220
  108.2 11.0 %collective-permute-done.16.refs_6_ = bf16[320,1280]{1,0:T(8,128)(2,1)S(1)} collective-permute-done((bf16[320,1280]{1,0:T(8,128)(2,1)}, bf16[320,1280]{1,0:T(8,128)(2,1)S(1)}, u32[]{:S(2)}, u32[]{:S(2)}) %collective-permute-start.16) | collective-permute-done | bytes 819232 | tf_op jit(solution)/shard_map/ppermute | solution.py:220
  119.2 3.2 %collective-permute-done.17.refs_7_ = bf16[320,1280]{1,0:T(8,128)(2,1)S(1)} collective-permute-done((bf16[320,1280]{1,0:T(8,128)(2,1)}, bf16[320,1280]{1,0:T(8,128)(2,1)S(1)}, u32[]{:S(2)}, u32[]{:S(2)}) %collective-permute-start.17) | collective-permute-done | bytes 819232 | tf_op jit(solution)/shard_map/ppermute | solution.py:220
  122.4 3.3 %collective-permute-start.23 = (bf16[320,1280]{1,0:T(8,128)(2,1)}, bf16[320,1280]{1,0:T(8,128)(2,1)}, u32[]{:S(2)}, u32[]{:S(2)}) collective-permute-start(bf16[320,1280]{1,0:T(8,128)(2,1)} %collective-permute-done.21.refs_5_), channel_id=1, source_target_pairs={{0,96},{32,0},{64,32},{96,64},{1,97},{33,1},{65,33},{97,65},{2,98}... | collective-permute-start | bytes 2457608 | tf_op jit(solution)/shard_map/ppermute | solution.py:220
  125.8 1.7 copy-done.2
  127.5 1.1 copy-done.8
  128.6 11.1 %expert_part.3 = (bf16[256,1280]{1,0:T(8,128)(2,1)S(1)}, bf16[256,1280]{1,0:T(8,128)(2,1)S(1)}, f32[2,1280]{1,0:T(2,128)S(1)}) custom-call(s32[4]{0:T(128)S(1)} %pad_add_fusion.where_ref.refs_0_, bf16[320,1280]{1,0:T(8,128)(2,1)} %bitcast.6.refs_1_, bf16[320,1280]{1,0:T(8,128)(2,1)} %collective-permute-done.9.refs_2_, bf16[320,1280]{1,0:T(8,128)(2,1)S(1)} %copy-done.8, ...), custom_call_target="tpu_custom_call" | custom-call | tf_op jit(solution)/shard_map/expert_part/pallas_call | solution.py:163
  139.8 0.8 copy-done.9
  140.6 0.8 copy-done.15
  141.5 2.9 %collective-permute-start.25 = (bf16[256,1280]{1,0:T(8,128)(2,1)}, bf16[256,1280]{1,0:T(8,128)(2,1)}, u32[]{:S(2)}, u32[]{:S(2)}) collective-permute-start(bf16[256,1280]{1,0:T(8,128)(2,1)} %copy-done.15), channel_id=1, source_target_pairs={{0,16},{16,0},{1,17},{17,1},{2,18},{18,2},{3,19},{19,3},{4,20},{20... | collective-permute-start | bytes 1966088 | tf_op jit(solution)/shard_map/ppermute | solution.py:220
  144.4 1.7 copy-done.3
  146.1 1.1 copy-done.5
  147.3 5.0 %expert_part.4 = f32[1,1280]{1,0:T(1,128)S(1)} custom-call(s32[4]{0:T(128)S(1)} %pad_add_fusion.where_ref.refs_0_, bf16[320,1280]{1,0:T(8,128)(2,1)S(1)} %bitcast.33, bf16[320,1280]{1,0:T(8,128)(2,1)} %collective-permute-done.20.refs_2_, bf16[320,1280]{1,0:T(8,128)(2,1)S(1)} %copy-done.5, bf16[320,1280]{1,0:T(8,128)(2,1)} %collective-permute-done.13.refs_4_, ...), custom_call_target="tpu_custom_call" | custom-call | tf_op jit(solution)/shard_map/expert_part/pallas_call | solution.py:163
  152.3 3.3 %collective-permute-done.22.refs_6_ = bf16[320,1280]{1,0:T(8,128)(2,1)} collective-permute-done((bf16[320,1280]{1,0:T(8,128)(2,1)}, bf16[320,1280]{1,0:T(8,128)(2,1)}, u32[]{:S(2)}, u32[]{:S(2)}) %collective-permute-start.22) | collective-permute-done | bytes 819232 | tf_op jit(solution)/shard_map/ppermute | solution.py:220
  155.6 2.0 collective-permute-done.23.refs_7_
  157.6 1.4 collective-permute-done.24.refs_8_
  159.0 10.4 %expert_part.5 = (bf16[256,1280]{1,0:T(8,128)(2,1)S(1)}, bf16[256,1280]{1,0:T(8,128)(2,1)}, f32[1,1280]{1,0:T(1,128)S(1)}) custom-call(s32[4]{0:T(128)S(1)} %pad_add_fusion.where_ref.refs_0_, bf16[320,1280]{1,0:T(8,128)(2,1)S(1)} %bitcast.34, bf16[320,1280]{1,0:T(8,128)(2,1)} %collective-permute-done.20.refs_2_, bf16[320,1280]{1,0:T(8,128)(2,1)S(1)} %copy-done.5, ...), custom_call_target="tpu_custom_call" | custom-call | tf_op jit(solution)/shard_map/expert_part/pallas_call | solution.py:163
  169.4 0.8 copy-done.11
  170.2 3.5 %collective-permute-start.26 = (bf16[256,1280]{1,0:T(8,128)(2,1)}, bf16[256,1280]{1,0:T(8,128)(2,1)S(1)}, u32[]{:S(2)}, u32[]{:S(2)}) collective-permute-start(bf16[256,1280]{1,0:T(8,128)(2,1)} %get-tuple-element.49), channel_id=1, source_target_pairs={{0,16},{16,0},{1,17},{17,1},{2,18},{18,2},{3,19},{19,3},{4,20},{20... | collective-permute-start | bytes 1966088 | tf_op jit(solution)/shard_map/ppermute | solution.py:220
  173.8 0.5 fusion.1
  174.6 9.2 %all_to_all.32 = f32[16,1,160]{2,1,0:T(1,128)S(1)} all-to-all(f32[16,1,160]{2,1,0:T(1,128)S(1)} %all_to_all.27), channel_id=1, replica_groups=mesh['x_lo'=2,'y'=4,'core'=2,'x_hi'=2,'z'=8] {'x_lo','y','core'}, dimensions={0} | all-to-all | bytes 20480 | tf_op jit(solution)/shard_map/all_to_all | solution.py:307
  183.8 0.7 all_to_all.24
  184.5 7.2 %all-to-all-start.3 = ((f32[16,1,10]{2,1,0:T(1,128)}), f32[16,1,10]{2,1,0:T(1,128)S(1)}, u32[]{:S(2)}, u32[]{:S(2)}) async-start(f32[16,1,10]{2,1,0:T(1,128)} %bitcast.14), calls=%async_computation.3 | async-start | bytes 16384 | tf_op jit(solution)/shard_map/all_to_all | solution.py:309
  191.7 1.1 copy-done.10
  192.8 1.1 copy-done.12
  193.9 3.3 %join.1 = bf16[256,5120]{1,0:T(8,128)(2,1)} custom-call(s32[4]{0:T(128)S(1)} %pad_add_fusion.where_ref.refs_0_, bf16[256,1280]{1,0:T(8,128)(2,1)S(1)} %copy-done.10, bf16[256,1280]{1,0:T(8,128)(2,1)S(1)} %copy-done.12, bf16[256,1280]{1,0:T(8,128)(2,1)} %collective-permute-done.25.refs_3_, bf16[256,1280]{1,0:T(8,128)(2,1)S(1)} %collective-permute-done.26.refs_4_), custom_call_target="tpu_custom_call" | custom-call | tf_op jit(solution)/shard_map/join/pallas_call | solution.py:202
  197.2 3.3 %all-to-all-done.3 = f32[16,1,10]{2,1,0:T(1,128)S(1)} async-done(((f32[16,1,10]{2,1,0:T(1,128)}), f32[16,1,10]{2,1,0:T(1,128)S(1)}, u32[]{:S(2)}, u32[]{:S(2)}) %all-to-all-start.3) | async-done | bytes 672 | tf_op jit(solution)/shard_map/all_to_all | solution.py:309
  200.7 0.5 fusion.6
  (63 shorter events, 1.0 us)
Async XLA Ops:
  0.6 7.7 %copy-start.18 = (s32[128,1]{0,1:T(1,128)S(1)}, s32[128,1]{0,1:T(1,128)}, u32[]{:S(2)}) copy-start(s32[128,1]{0,1:T(1,128)} %param.7) | copy-start | bytes 1540
  2.0 9.5 %collective-permute-start.3 = (bf16[128,1280]{1,0:T(8,128)(2,1)S(1)}, bf16[128,1280]{1,0:T(8,128)(2,1)S(1)}, u32[]{:S(2)}, u32[]{:S(2)}) collective-permute-start(bf16[128,1280]{1,0:T(8,128)(2,1)S(1)} %get-tuple-element.52), channel_id=1, source_target_pairs={{0,16},{16,0},{1,17},{17,1},{2,18},{18,2},{3,19},{19,3},{4,20},{20... | collective-permute-start | bytes 983048 | tf_op jit(solution)/shard_map/ppermute | solution.py:220
  5.3 10.5 %collective-permute-start.4 = (bf16[128,1280]{1,0:T(8,128)(2,1)S(1)}, bf16[128,1280]{1,0:T(8,128)(2,1)S(1)}, u32[]{:S(2)}, u32[]{:S(2)}) collective-permute-start(bf16[128,1280]{1,0:T(8,128)(2,1)S(1)} %get-tuple-element.29.t0), channel_id=1, source_target_pairs={{0,136},{8,128},{16,152},{24,144},{128,8},{136,0},{144,24},{152,16... | collective-permute-start | bytes 983048 | tf_op jit(solution)/shard_map/ppermute | solution.py:230
  6.1 17.0 %collective-permute-start.5 = (bf16[128,1280]{1,0:T(8,128)(2,1)S(1)}, bf16[128,1280]{1,0:T(8,128)(2,1)S(1)}, u32[]{:S(2)}, u32[]{:S(2)}) collective-permute-start(bf16[128,1280]{1,0:T(8,128)(2,1)S(1)} %get-tuple-element.52), channel_id=1, source_target_pairs={{0,152},{8,144},{16,136},{24,128},{128,24},{136,16},{144,8},{152,0... | collective-permute-start | bytes 983048 | tf_op jit(solution)/shard_map/ppermute | solution.py:230
  10.6 12.5 %collective-permute-start = (f32[8,128]{1,0:T(8,128)}, f32[8,128]{1,0:T(8,128)S(1)}, u32[]{:S(2)}, u32[]{:S(2)}) collective-permute-start(f32[8,128]{1,0:T(8,128)} %route.1.m0), channel_id=1, source_target_pairs={{0,16},{16,0},{1,17},{17,1},{2,18},{18,2},{3,19},{19,3},{4,20},{20... | collective-permute-start | bytes 12296 | tf_op jit(solution)/shard_map/ppermute | solution.py:220
  10.7 12.4 %collective-permute-start.1 = (f32[8,128]{1,0:T(8,128)}, f32[8,128]{1,0:T(8,128)S(1)}, u32[]{:S(2)}, u32[]{:S(2)}) collective-permute-start(f32[8,128]{1,0:T(8,128)} %route.1.m0), channel_id=1, source_target_pairs={{0,136},{8,128},{16,152},{24,144},{128,8},{136,0},{144,24},{152,16... | collective-permute-start | bytes 12296 | tf_op jit(solution)/shard_map/ppermute | solution.py:230
  11.5 12.0 %collective-permute-start.2 = (f32[8,128]{1,0:T(8,128)}, f32[8,128]{1,0:T(8,128)S(1)}, u32[]{:S(2)}, u32[]{:S(2)}) collective-permute-start(f32[8,128]{1,0:T(8,128)} %route.1.m0), channel_id=1, source_target_pairs={{0,152},{8,144},{16,136},{24,128},{128,24},{136,16},{144,8},{152,0... | collective-permute-start | bytes 12296 | tf_op jit(solution)/shard_map/ppermute | solution.py:230
  23.5 0.7 copy-start.13
  26.2 25.0 %copy-start.14 = (f32[8,128]{1,0:T(8,128)S(1)}, f32[8,128]{1,0:T(8,128)}, u32[]{:S(2)}) copy-start(f32[8,128]{1,0:T(8,128)} %route.1.m0) | copy-start | bytes 12292
  26.2 31.0 %all-to-all-start = ((bf16[8,40,1280]{2,1,0:T(8,128)(2,1)}), bf16[8,40,1280]{2,1,0:T(8,128)(2,1)}, u32[]{:S(2)}, u32[]{:S(2)}) async-start(bf16[8,40,1280]{2,1,0:T(8,128)(2,1)} %bitcast.5), calls=%async_computation | async-start | bytes 1638400 | tf_op jit(solution)/shard_map/all_to_all | solution.py:265
  32.8 3.8 %collective-permute-start.6 = (bf16[128,1280]{1,0:T(8,128)(2,1)S(1)}, bf16[128,1280]{1,0:T(8,128)(2,1)S(1)}, u32[]{:S(2)}, u32[]{:S(2)}) collective-permute-start(bf16[128,1280]{1,0:T(8,128)(2,1)S(1)} %get-tuple-element.28), channel_id=1, source_target_pairs={{0,16},{16,0},{1,17},{17,1},{2,18},{18,2},{3,19},{19,3},{4,20},{20... | collective-permute-start | bytes 983048 | tf_op jit(solution)/shard_map/ppermute | solution.py:220
  33.4 10.6 %collective-permute-start.7 = (bf16[128,1280]{1,0:T(8,128)(2,1)S(1)}, bf16[128,1280]{1,0:T(8,128)(2,1)S(1)}, u32[]{:S(2)}, u32[]{:S(2)}) collective-permute-start(bf16[128,1280]{1,0:T(8,128)(2,1)S(1)} %get-tuple-element.27.t0), channel_id=1, source_target_pairs={{0,136},{8,128},{16,152},{24,144},{128,8},{136,0},{144,24},{152,16... | collective-permute-start | bytes 983048 | tf_op jit(solution)/shard_map/ppermute | solution.py:230
  35.9 15.2 %collective-permute-start.8 = (bf16[128,1280]{1,0:T(8,128)(2,1)S(1)}, bf16[128,1280]{1,0:T(8,128)(2,1)S(1)}, u32[]{:S(2)}, u32[]{:S(2)}) collective-permute-start(bf16[128,1280]{1,0:T(8,128)(2,1)S(1)} %get-tuple-element.28), channel_id=1, source_target_pairs={{0,152},{8,144},{16,136},{24,128},{128,24},{136,16},{144,8},{152,0... | collective-permute-start | bytes 983048 | tf_op jit(solution)/shard_map/ppermute | solution.py:230
  36.4 29.4 %collective-permute-start.10 = (bf16[2560,256]{1,0:T(8,128)(2,1)}, bf16[2560,256]{1,0:T(8,128)(2,1)}, u32[]{:S(2)}, u32[]{:S(2)}) collective-permute-start(bf16[2560,256]{1,0:T(8,128)(2,1)} %bitcast.9.own_ref), channel_id=1, source_target_pairs={{0,16},{16,0},{1,17},{17,1},{2,18},{18,2},{3,19},{19,3},{4,20},{20... | collective-permute-start | bytes 3932168 | tf_op jit(solution)/shard_map/ppermute | solution.py:220
  51.1 12.5 %copy-start = (bf16[1,256,5120]{2,1,0:T(8,128)(2,1)S(1)}, bf16[1,256,5120]{2,1,0:T(8,128)(2,1)}, u32[]{:S(2)}) copy-start(bf16[1,256,5120]{2,1,0:T(8,128)(2,1)} %param.10) | copy-start | bytes 7864324
  52.3 0.9 copy-start.6
  57.1 27.8 %all-to-all-start.1 = ((bf16[8,40,1280]{2,1,0:T(8,128)(2,1)}), bf16[8,40,1280]{2,1,0:T(8,128)(2,1)S(1)}, u32[]{:S(2)}, u32[]{:S(2)}) async-start(bf16[8,40,1280]{2,1,0:T(8,128)(2,1)} %bitcast.35), calls=%async_computation.1 | async-start | bytes 1638400 | tf_op jit(solution)/shard_map/all_to_all | solution.py:265
  60.7 21.1 %collective-permute-start.9 = (bf16[320,1280]{1,0:T(8,128)(2,1)}, bf16[320,1280]{1,0:T(8,128)(2,1)}, u32[]{:S(2)}, u32[]{:S(2)}) collective-permute-start(bf16[320,1280]{1,0:T(8,128)(2,1)} %bitcast.6.refs_1_), channel_id=1, source_target_pairs={{0,32},{32,64},{64,96},{96,0},{1,33},{33,65},{65,97},{97,1},{2,34}... | collective-permute-start | bytes 2457608 | tf_op jit(solution)/shard_map/ppermute | solution.py:220
  62.1 19.7 %collective-permute-start.11 = (bf16[320,1280]{1,0:T(8,128)(2,1)}, bf16[320,1280]{1,0:T(8,128)(2,1)S(1)}, u32[]{:S(2)}, u32[]{:S(2)}) collective-permute-start(bf16[320,1280]{1,0:T(8,128)(2,1)} %bitcast.6.refs_1_), channel_id=1, source_target_pairs={{0,96},{32,0},{64,32},{96,64},{1,97},{33,1},{65,33},{97,65},{2,98}... | collective-permute-start | bytes 2457608 | tf_op jit(solution)/shard_map/ppermute | solution.py:220
  63.6 2.1 %copy-start.16 = (s32[640,1]{1,0:T(8,128)S(1)}, s32[640,1]{1,0:T(8,128)}, u32[]{:S(2)}) copy-start(s32[640,1]{1,0:T(8,128)} %constant.35.target_ref) | copy-start | bytes 7684
  64.8 22.9 %collective-permute-start.19 = (bf16[256,2560]{1,0:T(8,128)(2,1)}, bf16[256,2560]{1,0:T(8,128)(2,1)}, u32[]{:S(2)}, u32[]{:S(2)}) collective-permute-start(bf16[256,2560]{1,0:T(8,128)(2,1)} %slice_select_fusion), channel_id=1, source_target_pairs={{0,16},{16,0},{1,17},{17,1},{2,18},{18,2},{3,19},{19,3},{4,20},{20... | collective-permute-start | bytes 3932168 | tf_op jit(solution)/shard_map/ppermute | solution.py:220
  65.7 21.9 %collective-permute-start.15 = (bf16[320,1280]{1,0:T(8,128)(2,1)}, bf16[320,1280]{1,0:T(8,128)(2,1)}, u32[]{:S(2)}, u32[]{:S(2)}) collective-permute-start(bf16[320,1280]{1,0:T(8,128)(2,1)} %bitcast.6.refs_1_), channel_id=1, source_target_pairs={{0,128},{128,0},{1,129},{129,1},{2,130},{130,2},{3,131},{131,3},{4... | collective-permute-start | bytes 2457608 | tf_op jit(solution)/shard_map/ppermute | solution.py:220
  70.2 1.5 copy-start.1
  81.7 20.0 %collective-permute-start.14 = (bf16[320,1280]{1,0:T(8,128)(2,1)}, bf16[320,1280]{1,0:T(8,128)(2,1)}, u32[]{:S(2)}, u32[]{:S(2)}) collective-permute-start(bf16[320,1280]{1,0:T(8,128)(2,1)} %collective-permute-done.9.refs_2_), channel_id=1, source_target_pairs={{0,32},{32,64},{64,96},{96,0},{1,33},{33,65},{65,97},{97,1},{2,34}... | collective-permute-start | bytes 2457608 | tf_op jit(solution)/shard_map/ppermute | solution.py:220
  81.7 0.9 copy-start.7
  84.9 19.9 %collective-permute-start.12 = (bf16[320,1280]{1,0:T(8,128)(2,1)S(1)}, bf16[320,1280]{1,0:T(8,128)(2,1)S(1)}, u32[]{:S(2)}, u32[]{:S(2)}) collective-permute-start(bf16[320,1280]{1,0:T(8,128)(2,1)S(1)} %bitcast.30), channel_id=1, source_target_pairs={{0,96},{32,0},{64,32},{96,64},{1,97},{33,1},{65,33},{97,65},{2,98}... | collective-permute-start | bytes 2457608 | tf_op jit(solution)/shard_map/ppermute | solution.py:220
  87.7 31.5 %collective-permute-start.16 = (bf16[320,1280]{1,0:T(8,128)(2,1)}, bf16[320,1280]{1,0:T(8,128)(2,1)S(1)}, u32[]{:S(2)}, u32[]{:S(2)}) collective-permute-start(bf16[320,1280]{1,0:T(8,128)(2,1)} %collective-permute-done.15.refs_5_), channel_id=1, source_target_pairs={{0,32},{32,64},{64,96},{96,0},{1,33},{33,65},{65,97},{97,1},{2,34}... | collective-permute-start | bytes 2457608 | tf_op jit(solution)/shard_map/ppermute | solution.py:220
  87.7 31.5 %collective-permute-start.21 = (bf16[320,1280]{1,0:T(8,128)(2,1)S(1)}, bf16[320,1280]{1,0:T(8,128)(2,1)}, u32[]{:S(2)}, u32[]{:S(2)}) collective-permute-start(bf16[320,1280]{1,0:T(8,128)(2,1)S(1)} %bitcast.31), channel_id=1, source_target_pairs={{0,128},{128,0},{1,129},{129,1},{2,130},{130,2},{3,131},{131,3},{4... | collective-permute-start | bytes 2457608 | tf_op jit(solution)/shard_map/ppermute | solution.py:220
  87.7 34.8 %collective-permute-start.17 = (bf16[320,1280]{1,0:T(8,128)(2,1)}, bf16[320,1280]{1,0:T(8,128)(2,1)S(1)}, u32[]{:S(2)}, u32[]{:S(2)}) collective-permute-start(bf16[320,1280]{1,0:T(8,128)(2,1)} %collective-permute-done.15.refs_5_), channel_id=1, source_target_pairs={{0,96},{32,0},{64,32},{96,64},{1,97},{33,1},{65,33},{97,65},{2,98}... | collective-permute-start | bytes 2457608 | tf_op jit(solution)/shard_map/ppermute | solution.py:220
  101.7 24.0 %collective-permute-start.18 = (bf16[320,1280]{1,0:T(8,128)(2,1)}, bf16[320,1280]{1,0:T(8,128)(2,1)S(1)}, u32[]{:S(2)}, u32[]{:S(2)}) collective-permute-start(bf16[320,1280]{1,0:T(8,128)(2,1)} %collective-permute-done.14.refs_4_), channel_id=1, source_target_pairs={{0,128},{128,0},{1,129},{129,1},{2,130},{130,2},{3,131},{131,3},{4... | collective-permute-start | bytes 2457608 | tf_op jit(solution)/shard_map/ppermute | solution.py:220
  104.8 35.0 %copy-start.4 = (bf16[320,1280]{1,0:T(8,128)(2,1)}, bf16[320,1280]{1,0:T(8,128)(2,1)S(1)}, u32[]{:S(2)}) copy-start(bf16[320,1280]{1,0:T(8,128)(2,1)S(1)} %collective-permute-done.12.refs_3_) | copy-start | bytes 2457604
  104.8 36.7 %collective-permute-start.13 = (bf16[320,1280]{1,0:T(8,128)(2,1)S(1)}, bf16[320,1280]{1,0:T(8,128)(2,1)}, u32[]{:S(2)}, u32[]{:S(2)}) collective-permute-start(bf16[320,1280]{1,0:T(8,128)(2,1)S(1)} %collective-permute-done.12.refs_3_), channel_id=1, source_target_pairs={{0,96},{32,0},{64,32},{96,64},{1,97},{33,1},{65,33},{97,65},{2,98}... | collective-permute-start | bytes 2457608 | tf_op jit(solution)/shard_map/ppermute | solution.py:220
  119.2 25.2 %collective-permute-start.20 = (bf16[320,1280]{1,0:T(8,128)(2,1)S(1)}, bf16[320,1280]{1,0:T(8,128)(2,1)}, u32[]{:S(2)}, u32[]{:S(2)}) collective-permute-start(bf16[320,1280]{1,0:T(8,128)(2,1)S(1)} %bitcast.32), channel_id=1, source_target_pairs={{0,32},{32,64},{64,96},{96,0},{1,33},{33,65},{65,97},{97,1},{2,34}... | collective-permute-start | bytes 2457608 | tf_op jit(solution)/shard_map/ppermute | solution.py:220
  119.2 36.4 %collective-permute-start.22 = (bf16[320,1280]{1,0:T(8,128)(2,1)}, bf16[320,1280]{1,0:T(8,128)(2,1)}, u32[]{:S(2)}, u32[]{:S(2)}) collective-permute-start(bf16[320,1280]{1,0:T(8,128)(2,1)} %collective-permute-done.21.refs_5_), channel_id=1, source_target_pairs={{0,32},{32,64},{64,96},{96,0},{1,33},{33,65},{65,97},{97,1},{2,34}... | collective-permute-start | bytes 2457608 | tf_op jit(solution)/shard_map/ppermute | solution.py:220
  122.4 35.1 %collective-permute-start.23 = (bf16[320,1280]{1,0:T(8,128)(2,1)}, bf16[320,1280]{1,0:T(8,128)(2,1)}, u32[]{:S(2)}, u32[]{:S(2)}) collective-permute-start(bf16[320,1280]{1,0:T(8,128)(2,1)} %collective-permute-done.21.refs_5_), channel_id=1, source_target_pairs={{0,96},{32,0},{64,32},{96,64},{1,97},{33,1},{65,33},{97,65},{2,98}... | collective-permute-start | bytes 2457608 | tf_op jit(solution)/shard_map/ppermute | solution.py:220
  125.8 1.7 copy-start.2
  127.5 1.1 copy-start.8
  139.8 0.8 copy-start.9
  140.6 0.8 copy-start.15
  141.5 17.5 %collective-permute-start.24 = (bf16[320,1280]{1,0:T(8,128)(2,1)}, bf16[320,1280]{1,0:T(8,128)(2,1)}, u32[]{:S(2)}, u32[]{:S(2)}) collective-permute-start(bf16[320,1280]{1,0:T(8,128)(2,1)} %collective-permute-done.13.refs_4_), channel_id=1, source_target_pairs={{0,128},{128,0},{1,129},{129,1},{2,130},{130,2},{3,131},{131,3},{4... | collective-permute-start | bytes 2457608 | tf_op jit(solution)/shard_map/ppermute | solution.py:220
  141.5 50.2 %collective-permute-start.25 = (bf16[256,1280]{1,0:T(8,128)(2,1)}, bf16[256,1280]{1,0:T(8,128)(2,1)}, u32[]{:S(2)}, u32[]{:S(2)}) collective-permute-start(bf16[256,1280]{1,0:T(8,128)(2,1)} %copy-done.15), channel_id=1, source_target_pairs={{0,16},{16,0},{1,17},{17,1},{2,18},{18,2},{3,19},{19,3},{4,20},{20... | collective-permute-start | bytes 1966088 | tf_op jit(solution)/shard_map/ppermute | solution.py:220
  144.4 1.7 copy-start.3
  146.1 1.1 copy-start.5
  152.3 21.5 %copy-start.19 = (s32[2,2,80]{2,1,0:T(2,128)S(1)}, s32[2,2,80]{2,1,0:T(2,128)}, u32[]{:S(2)}) copy-start(s32[2,2,80]{2,1,0:T(2,128)} %constant.37) | copy-start | bytes 3844
  169.4 0.8 copy-start.11
  170.2 21.5 %collective-permute-start.26 = (bf16[256,1280]{1,0:T(8,128)(2,1)}, bf16[256,1280]{1,0:T(8,128)(2,1)S(1)}, u32[]{:S(2)}, u32[]{:S(2)}) collective-permute-start(bf16[256,1280]{1,0:T(8,128)(2,1)} %get-tuple-element.49), channel_id=1, source_target_pairs={{0,16},{16,0},{1,17},{17,1},{2,18},{18,2},{3,19},{19,3},{4,20},{20... | collective-permute-start | bytes 1966088 | tf_op jit(solution)/shard_map/ppermute | solution.py:220
  184.5 16.0 %all-to-all-start.3 = ((f32[16,1,10]{2,1,0:T(1,128)}), f32[16,1,10]{2,1,0:T(1,128)S(1)}, u32[]{:S(2)}, u32[]{:S(2)}) async-start(f32[16,1,10]{2,1,0:T(1,128)} %bitcast.14), calls=%async_computation.3 | async-start | bytes 16384 | tf_op jit(solution)/shard_map/all_to_all | solution.py:309
  191.7 1.1 copy-start.10
  192.8 1.1 copy-start.12
  193.9 6.8 %copy-start.17 = (f32[128]{0:T(128)S(1)}, f32[128]{0:T(128)}, u32[]{:S(2)}) copy-start(f32[128]{0:T(128)} %param.8) | copy-start | bytes 1540
